TPU v7x, 128 devices: a whole 4x4x4 slice. The times are simulated.
128 devices in a mesh: row: 8 (over x, core), col: 16 (over z, y).
Axes of the slice: x: 4, y: 4, z: 4, core: 2. Of those that a mesh axis runs over, the one named last changes fastest.
Arguments:
- object_field: float32 [2, 8192, 4096], P(None, 'row', 'col'), may hold values from -5 to 5
- probe_modes: float32 [2, 3, 256, 256], replicated, may hold values from -6 to 6
- amplitudes: float32 [8, 16, 8, 256, 256], P('row', 'col'), may hold values from 0 to 3
- scan_offsets: int32 [8, 16, 8, 2], P('row', 'col'), may hold values from -128 to 8063, as said below
- slot_counts: int32 [8, 16], P('row', 'col'), may hold values from 1 to 8, as said below
Outputs:
- new_object: float32 [2, 8192, 4096], P(None, 'row', 'col')
- new_probe: float32 [2, 3, 256, 256], replicated
Inputs may be any that keep to these rules, and one draw needn't show every extreme that they name: Each slot's window centre, scan_offsets + 128, lies in the tile of the device that holds the slot; slots at or past the tile's count carry offsets of the same kind but are not live. `slot_counts`: in every draw some tile has all 8 slots live and another has one.
All inputs are finite; a program needn't handle non-finite values.
Results may differ from a plain program's by a relative error of at most 0.0003.
Values sent between devices are 32-bit elements; how exact they have to be, the bound alone decides.
A program may use at most 128 MiB of HBM per device.

v0:
```python
import math

import jax
import jax.numpy as jnp
from jax import lax
from jax.sharding import PartitionSpec as P


def passed_along(block, axis, distance):
    devices = range(lax.axis_size(axis))
    route = [(i - distance, i) for i in devices if i - distance in devices]
    return lax.ppermute(block, axis, route)


def extended(value, sides, width):
    for axis, dim in sides:
        peers, length = (lax.axis_size(axis), value.shape[dim])
        up = [(i, (i + 1) % peers) for i in range(peers - 1)]
        down = [(j, i) for i, j in up]
        last = lax.slice_in_dim(value, length - width, length, axis=dim)
        first = lax.slice_in_dim(value, 0, width, axis=dim)
        before = lax.ppermute(last, axis, up)
        after = lax.ppermute(first, axis, down)
        value = jnp.concatenate([before, value, after], axis=dim)
    return value


def dft_tables(length):
    index = lax.iota(jnp.int32, length)
    product = index[:, None] * index[None, :] % length
    angle = product.astype(jnp.float32) * (2.0 * math.pi / length)
    factor = 1.0 / math.sqrt(length)
    return (jnp.cos(angle) * factor, -jnp.sin(angle) * factor)


def transform(real_part, imag_part, cosine, sine):
    highest = lax.Precision.HIGHEST
    left_real = jnp.einsum("kn,cmnj->cmkj", cosine, real_part, precision=highest) - jnp.einsum(
        "kn,cmnj->cmkj", sine, imag_part, precision=highest
    )
    left_imag = jnp.einsum("kn,cmnj->cmkj", cosine, imag_part, precision=highest) + jnp.einsum(
        "kn,cmnj->cmkj", sine, real_part, precision=highest
    )
    out_real = jnp.einsum("cmkn,nj->cmkj", left_real, cosine, precision=highest) - jnp.einsum(
        "cmkn,nj->cmkj", left_imag, sine, precision=highest
    )
    out_imag = jnp.einsum("cmkn,nj->cmkj", left_real, sine, precision=highest) + jnp.einsum(
        "cmkn,nj->cmkj", left_imag, cosine, precision=highest
    )
    return (out_real, out_imag)


def send_cols(strip, offset):
    return passed_along(strip, "col", offset)


def send_rows(strip, offset):
    return passed_along(strip, "row", offset)


def on_device(object_field, probe_modes, amplitudes, scan_offsets, slot_counts):
    length = probe_modes.shape[-1]
    half = length // 2
    tile_rows = object_field.shape[1]
    tile_cols = object_field.shape[2]
    capacity = scan_offsets.shape[2]
    padded = extended(object_field, (("row", 1), ("col", 2)), half)
    anchor_rows = lax.axis_index("row") * tile_rows
    anchor_cols = lax.axis_index("col") * tile_cols
    offsets = scan_offsets.reshape(capacity, 2)
    tops = offsets[:, 0] - anchor_rows + half
    lefts = offsets[:, 1] - anchor_cols + half
    start_zero = jnp.zeros((), jnp.int32)

    def window_at(top, left):
        return lax.dynamic_slice(padded, (start_zero, top, left), (2, length, length))

    windows = jax.vmap(window_at)(tops, lefts)
    patch_real = windows[:, 0][:, None]
    patch_imag = windows[:, 1][:, None]
    probe_real = probe_modes[0][None]
    probe_imag = probe_modes[1][None]
    wave_real = probe_real * patch_real - probe_imag * patch_imag
    wave_imag = probe_real * patch_imag + probe_imag * patch_real
    cosine, sine = dft_tables(length)
    spec_real, spec_imag = transform(wave_real, wave_imag, cosine, sine)
    intensity = jnp.sum(spec_real * spec_real + spec_imag * spec_imag, axis=1)
    measured = amplitudes.reshape(capacity, length, length)
    active = (lax.iota(jnp.int32, capacity) < slot_counts.reshape(())).astype(jnp.float32)
    ratio = (1.0 - measured / jnp.sqrt(jnp.maximum(intensity, 1.0))) * active[:, None, None]
    chi_real, chi_imag = transform(
        spec_real * ratio[:, None], spec_imag * ratio[:, None], cosine, -sine
    )
    grad_real = jnp.sum(probe_real * chi_real + probe_imag * chi_imag, axis=1)
    grad_imag = jnp.sum(probe_real * chi_imag - probe_imag * chi_real, axis=1)
    patch_grads = jnp.stack([grad_real, grad_imag], axis=1)

    def deposit(slot, total):
        start = (start_zero, tops[slot], lefts[slot])
        current = lax.dynamic_slice(total, start, (2, length, length))
        return lax.dynamic_update_slice(total, current + patch_grads[slot], start)

    gradient = lax.fori_loop(0, capacity, deposit, jnp.zeros_like(padded))
    from_right = send_cols(gradient[:, :, :half], -1)
    from_left = send_cols(gradient[:, :, tile_cols + half :], 1)
    gradient = gradient.at[:, :, tile_cols : tile_cols + half].add(from_right)
    gradient = gradient.at[:, :, half : 2 * half].add(from_left)
    from_below = send_rows(gradient[:, :half, half : tile_cols + half], -1)
    from_above = send_rows(gradient[:, tile_rows + half :, half : tile_cols + half], 1)
    gradient = gradient.at[:, tile_rows : tile_rows + half, half : tile_cols + half].add(from_below)
    gradient = gradient.at[:, half : 2 * half, half : tile_cols + half].add(from_above)
    interior = gradient[:, half : tile_rows + half, half : tile_cols + half]
    new_object = object_field - 0.25 * interior
    mode_real = jnp.sum(patch_real * chi_real + patch_imag * chi_imag, axis=0)
    mode_imag = jnp.sum(patch_real * chi_imag - patch_imag * chi_real, axis=0)
    local_probe = jnp.stack([mode_real, mode_imag])
    members = lax.axis_size("row") * lax.axis_size("col")
    factor = 0.5 / math.sqrt(members * capacity)
    total = lax.psum(local_probe, ("row", "col"))
    new_probe = probe_modes - factor * total
    return (new_object, new_probe)


def solution(mesh):
    placed = (
        P(None, "row", "col"),
        P(),
        P("row", "col", None, None, None),
        P("row", "col", None, None),
        P("row", "col"),
    )
    return jax.shard_map(
        on_device,
        mesh=mesh,
        in_specs=placed,
        out_specs=(P(None, "row", "col"), P()),
        check_vma=False,
    )
```

profile of v0, /device:TPU:1, one launch (start us, length us, event | category | flops | bytes accessed | tf_op | source)
XLA Modules:
  0.0 663.1 jit_solution(11022421115243410710)
XLA Ops:
  8.4 4.5 collective-permute-start
  23.8 4.3 collective-permute-start.2
  30.2 21.8 %collective-permute-done.2 = f32[2,1280,128]{2,1,0:T(8,128)} collective-permute-done((f32[2,1280,128]{2,1,0:T(8,128)}, f32[2,1280,128]{2,1,0:T(8,128)}, u32[]{:S(2)}, u32[]{:S(2)}) %collective-permute-start.2) | collective-permute-done | bytes 1310752 | tf_op jit(solution)/shard_map/ppermute | solution.py:22
  52.1 5.1 collective-permute-done.3
  57.2 5.4 pad_maximum_fusion
  62.6 32.5 %while.19 = (s32[]{:T(128)}, f32[2,1280,512]{2,1,0:T(8,128)}, s32[8,3]{0,1:T(4,128)S(1)}, f32[8,2,256,256]{3,2,1,0:T(8,128)}, s32[]{:T(128)}) while((s32[]{:T(128)}, f32[2,1280,512]{2,1,0:T(8,128)}, s32[8,3]{0,1:T(4,128)S(1)}, f32[8,2,256,256]{3,2,1,0:T(8,128)}, s32[]{:T(128)}) %tuple.76), condition=%wide.while_cond.4, body=%wide.while_body.4.sunk | while | flops 2 | bytes 1050217 | solution.py:76
  63.2 3.5 bitcast_dynamic-update-slice_fusion.2
  67.3 3.5 bitcast_dynamic-update-slice_fusion.2
  71.3 3.5 bitcast_dynamic-update-slice_fusion.2
  75.4 3.5 bitcast_dynamic-update-slice_fusion.2
  79.4 3.5 bitcast_dynamic-update-slice_fusion.2
  83.5 3.5 bitcast_dynamic-update-slice_fusion.2
  87.6 3.5 bitcast_dynamic-update-slice_fusion.2
  91.7 3.5 bitcast_dynamic-update-slice_fusion.2
  97.9 11.6 %fusion.18 = f32[8,3,256,256]{3,2,1,0:T(8,128)S(1)} fusion(f32[8,256,256]{2,1,0:T(8,128)S(1)} %get-tuple-element.184, f32[3,256,256]{2,1,0:T(8,128)S(1)} %get-tuple-element.190, f32[8,256,256]{2,1,0:T(8,128)S(1)} %get-tuple-element.183, f32[3,256,256]{2,1,0:T(8,128)S(1)} %get-tuple-element.189), kind=kOutput, calls=%fused_computation.28 | convolution fusion | flops 4837605376 | bytes 12058624 | tf_op jit(solution)/shard_map/kn,cmnj->cmkj/dot_general | solution.py:41
  109.5 11.9 %fusion.16 = f32[8,3,256,256]{3,2,1,0:T(8,128)S(1)} fusion(f32[8,256,256]{2,1,0:T(8,128)S(1)} %get-tuple-element.184, f32[3,256,256]{2,1,0:T(8,128)S(1)} %get-tuple-element.190, f32[8,256,256]{2,1,0:T(8,128)S(1)} %get-tuple-element.183, f32[3,256,256]{2,1,0:T(8,128)S(1)} %get-tuple-element.189), kind=kOutput, calls=%fused_computation.25 | convolution fusion | flops 4837539840 | bytes 12058624 | tf_op jit(solution)/shard_map/kn,cmnj->cmkj/dot_general | solution.py:41
  121.5 13.9 %fusion.8 = f32[8,3,256,256]{3,2,1,0:T(8,128)} fusion(f32[8,3,256,256]{3,2,1,0:T(8,128)S(1)} %fusion.16, f32[8,3,256,256]{3,2,1,0:T(8,128)S(1)} %fusion.18), kind=kOutput, calls=%fused_computation.11 | convolution fusion | flops 4834394112 | bytes 18874368 | tf_op jit(solution)/shard_map/cmkn,nj->cmkj/dot_general | solution.py:47
  135.4 14.1 %fusion.10 = f32[8,3,256,256]{3,2,1,0:T(8,128)} fusion(f32[8,3,256,256]{3,2,1,0:T(8,128)S(1)} %fusion.16, f32[8,3,256,256]{3,2,1,0:T(8,128)S(1)} %fusion.18), kind=kOutput, calls=%fused_computation.13 | convolution fusion | flops 4834459648 | bytes 18874368 | tf_op jit(solution)/shard_map/cmkn,nj->cmkj/dot_general | solution.py:44
  149.4 11.1 %fusion.17 = f32[8,3,256,256]{3,2,1,0:T(8,128)S(1)} fusion(f32[8,256,256]{2,1,0:T(8,128)S(1)} %get-tuple-element.184, f32[3,256,256]{2,1,0:T(8,128)S(1)} %get-tuple-element.190, f32[8,256,256]{2,1,0:T(8,128)S(1)} %get-tuple-element.183, f32[3,256,256]{2,1,0:T(8,128)S(1)} %get-tuple-element.189), kind=kOutput, calls=%fused_computation.26 | convolution fusion | flops 4837605376 | bytes 12058624 | tf_op jit(solution)/shard_map/kn,cmnj->cmkj/dot_general | solution.py:38
  160.6 14.1 %fusion.19 = f32[8,3,256,256]{3,2,1,0:T(8,128)} fusion(f32[8,256,256]{2,1,0:T(8,128)S(1)} %get-tuple-element.184, f32[3,256,256]{2,1,0:T(8,128)S(1)} %get-tuple-element.190, f32[8,256,256]{2,1,0:T(8,128)S(1)} %get-tuple-element.183, f32[3,256,256]{2,1,0:T(8,128)S(1)} %get-tuple-element.189), kind=kOutput, calls=%fused_computation.29 | convolution fusion | flops 4837539840 | bytes 12058624 | tf_op jit(solution)/shard_map/kn,cmnj->cmkj/dot_general | solution.py:38
  174.7 16.0 %fusion.56 = f32[8,3,256,256]{3,2,1,0:T(8,128)S(1)} fusion(f32[8,3,256,256]{3,2,1,0:T(8,128)} %fusion.10, f32[8,3,256,256]{3,2,1,0:T(8,128)} %fusion.19, f32[8,3,256,256]{3,2,1,0:T(8,128)S(1)} %fusion.17), kind=kOutput, calls=%fused_computation.68 | convolution fusion | flops 4835966976 | bytes 25165824 | tf_op jit(solution)/shard_map/cmkn,nj->cmkj/dot_general | solution.py:44
  190.8 18.6 %add_reduce_fusion.2 = (f32[8,256,256]{2,1,0:T(8,128)S(1)}, f32[8,3,256,256]{3,2,1,0:T(8,128)}) fusion(f32[8,3,256,256]{3,2,1,0:T(8,128)S(1)} %fusion.56, f32[8,3,256,256]{3,2,1,0:T(8,128)} %fusion.8, f32[8,3,256,256]{3,2,1,0:T(8,128)} %fusion.19, f32[8,3,256,256]{3,2,1,0:T(8,128)} %copy-done.1), kind=kOutput, calls=%fused_computation.23 | convolution fusion | flops 4841799680 | bytes 33554432 | tf_op jit(solution)/shard_map/cmkn,nj->cmkj/dot_general | solution.py:47
  211.6 14.0 %fusion.24 = f32[8,3,256,256]{3,2,1,0:T(8,128)} fusion(f32[8,3,256,256]{3,2,1,0:T(8,128)S(1)} %fusion.56, f32[8,256,256]{2,1,0:T(8,128)S(1)} %fusion.70), kind=kOutput, calls=%fused_computation.34 | convolution fusion | flops 4834525184 | bytes 14680064 | tf_op jit(solution)/shard_map/kn,cmnj->cmkj/dot_general | solution.py:41
  225.6 14.3 %fusion.20 = f32[8,3,256,256]{3,2,1,0:T(8,128)} fusion(f32[8,3,256,256]{3,2,1,0:T(8,128)S(1)} %bitcast.123, f32[8,256,256]{2,1,0:T(8,128)S(1)} %fusion.70), kind=kOutput, calls=%fused_computation.30 | convolution fusion | flops 4834394112 | bytes 14680064 | tf_op jit(solution)/shard_map/kn,cmnj->cmkj/dot_general | solution.py:41
  239.9 10.9 %fusion.22 = f32[8,3,256,256]{3,2,1,0:T(8,128)S(1)} fusion(f32[8,3,256,256]{3,2,1,0:T(8,128)S(1)} %bitcast.123, f32[8,256,256]{2,1,0:T(8,128)S(1)} %fusion.70), kind=kOutput, calls=%fused_computation.32 | convolution fusion | flops 4834525184 | bytes 14680064 | tf_op jit(solution)/shard_map/kn,cmnj->cmkj/dot_general | solution.py:38
  250.9 13.9 %fusion.26 = f32[8,3,256,256]{3,2,1,0:T(8,128)} fusion(f32[8,3,256,256]{3,2,1,0:T(8,128)S(1)} %fusion.56, f32[8,256,256]{2,1,0:T(8,128)S(1)} %fusion.70), kind=kOutput, calls=%fused_computation.36 | convolution fusion | flops 4834394112 | bytes 14680064 | tf_op jit(solution)/shard_map/kn,cmnj->cmkj/dot_general | solution.py:38
  264.8 16.1 %fusion = f32[8,3,256,256]{3,2,1,0:T(8,128)} fusion(f32[8,3,256,256]{3,2,1,0:T(8,128)} %fusion.20, f32[8,3,256,256]{3,2,1,0:T(8,128)S(1)} %bitcast.127), kind=kOutput, calls=%fused_computation.3 | convolution fusion | flops 4834394112 | bytes 18874368 | tf_op jit(solution)/shard_map/cmkn,nj->cmkj/dot_general | solution.py:47
  280.9 14.3 %fusion.2 = f32[8,3,256,256]{3,2,1,0:T(8,128)} fusion(f32[8,3,256,256]{3,2,1,0:T(8,128)S(1)} %bitcast.129, f32[8,3,256,256]{3,2,1,0:T(8,128)S(1)} %bitcast.127), kind=kOutput, calls=%fused_computation.5 | convolution fusion | flops 4834525184 | bytes 18874368 | tf_op jit(solution)/shard_map/cmkn,nj->cmkj/dot_general | solution.py:44
  295.1 15.7 %fusion.62 = f32[8,3,256,256]{3,2,1,0:T(8,128)} fusion(f32[8,3,256,256]{3,2,1,0:T(8,128)} %fusion.2, f32[8,3,256,256]{3,2,1,0:T(8,128)S(1)} %bitcast.125, f32[8,3,256,256]{3,2,1,0:T(8,128)S(1)} %fusion.22), kind=kOutput, calls=%fused_computation.70 | convolution fusion | flops 4835966976 | bytes 25165824 | tf_op jit(solution)/shard_map/cmkn,nj->cmkj/dot_general | solution.py:44
  310.9 23.3 %add_reduce_fusion = (f32[3,256,256]{2,1,0:T(8,128)S(1)}, f32[3,256,256]{2,1,0:T(8,128)S(1)}, f32[8,256,256]{2,1,0:T(8,128)}, f32[8,256,256]{2,1,0:T(8,128)}) fusion(f32[8,3,256,256]{3,2,1,0:T(8,128)} %fusion.62, f32[8,256,256]{2,1,0:T(8,128)S(1)} %get-tuple-element.184, f32[8,256,256]{2,1,0:T(8,128)S(1)} %get-tuple-element.183, ...), kind=kOutput, calls=%fused_computation.20 | convolution fusion | flops 4859822080 | bytes 36700160 | tf_op jit(solution)/shard_map/cmkn,nj->cmkj/dot_general | solution.py:47
  334.1 4.7 pad_maximum_fusion.1
  341.8 105.6 %while.18 = (s32[]{:T(128)}, f32[2,1280,512]{2,1,0:T(8,128)}, s32[8]{0:T(128)S(1)}, s32[8]{0:T(128)S(1)}, f32[8,2,256,256]{3,2,1,0:T(8,128)}, /*index=5*/s32[]{:T(128)}, s32[]{:T(128)}, s32[]{:T(128)}, s32[]{:T(128)}) while((s32[]{:T(128)}, f32[2,1280,512]{2,1,0:T(8,128)}, s32[8]{0:T(128)S(1)}, s32[8]{0:T(128)S(1)}, ...), condition=%wide.region_4.5_spmd, body=%wide.region_3.4_spmd.sunk | while | flops 131080 | bytes 2621641 | solution.py:103
  348.4 6.7 %dynamic_update_slice.8 = f32[2,1280,512]{2,1,0:T(8,128)} dynamic-update-slice(f32[2,1280,512]{2,1,0:T(8,128)} %get-tuple-element.282, f32[2,256,256]{2,1,0:T(8,128)S(1)} %bitcast_add_fusion.2, s32[]{:T(128)} %constant.182.clone.1..sunk, s32[]{:T(128)S(6)} %select_n.136, s32[]{:T(128)S(6)} %select_n.137) | dynamic-update-slice | bytes 1048580 | tf_op jit(solution)/shard_map/while/body/eval_jaxpr/dynamic_update_slice | solution.py:101
  361.7 6.5 dynamic_update_slice.8
  374.8 6.8 %dynamic_update_slice.8 = f32[2,1280,512]{2,1,0:T(8,128)} dynamic-update-slice(f32[2,1280,512]{2,1,0:T(8,128)} %get-tuple-element.282, f32[2,256,256]{2,1,0:T(8,128)S(1)} %bitcast_add_fusion.2, s32[]{:T(128)} %constant.182.clone.1..sunk, s32[]{:T(128)S(6)} %select_n.136, s32[]{:T(128)S(6)} %select_n.137) | dynamic-update-slice | bytes 1048580 | tf_op jit(solution)/shard_map/while/body/eval_jaxpr/dynamic_update_slice | solution.py:101
  388.2 6.8 %dynamic_update_slice.8 = f32[2,1280,512]{2,1,0:T(8,128)} dynamic-update-slice(f32[2,1280,512]{2,1,0:T(8,128)} %get-tuple-element.282, f32[2,256,256]{2,1,0:T(8,128)S(1)} %bitcast_add_fusion.2, s32[]{:T(128)} %constant.182.clone.1..sunk, s32[]{:T(128)S(6)} %select_n.136, s32[]{:T(128)S(6)} %select_n.137) | dynamic-update-slice | bytes 1048580 | tf_op jit(solution)/shard_map/while/body/eval_jaxpr/dynamic_update_slice | solution.py:101
  401.5 6.5 dynamic_update_slice.8
  414.6 6.5 dynamic_update_slice.8
  427.8 6.5 dynamic_update_slice.8
  440.9 6.6 dynamic_update_slice.8
  450.1 27.8 %collective-permute-done.4 = f32[2,1280,128]{2,1,0:T(8,128)S(1)} collective-permute-done((f32[2,1280,128]{2,1,0:T(8,128)S(1)}, f32[2,1280,128]{2,1,0:T(8,128)S(1)}, u32[]{:S(2)}, u32[]{:S(2)}) %collective-permute-start.4) | collective-permute-done | bytes 1310752 | tf_op jit(solution)/shard_map/ppermute | solution.py:12
  478.0 3.6 fusion.182
  481.6 3.2 collective-permute-start.5
  486.1 24.8 %collective-permute-done.5 = f32[2,1280,128]{2,1,0:T(8,128)} collective-permute-done((f32[2,1280,128]{2,1,0:T(8,128)}, f32[2,1280,128]{2,1,0:T(8,128)}, u32[]{:S(2)}, u32[]{:S(2)}) %collective-permute-start.5) | collective-permute-done | bytes 1310752 | tf_op jit(solution)/shard_map/ppermute | solution.py:12
  516.8 15.4 %collective-permute-done.6 = f32[2,128,256]{2,1,0:T(8,128)S(1)} collective-permute-done((f32[2,128,256]{2,1,0:T(8,128)S(1)}, f32[2,128,256]{2,1,0:T(8,128)S(1)}, u32[]{:S(2)}, u32[]{:S(2)}) %collective-permute-start.6) | collective-permute-done | bytes 262176 | tf_op jit(solution)/shard_map/ppermute | solution.py:12
  536.0 111.9 %all-reduce.2.cloned.1.call-done = f32[2,3,256,256]{3,2,1,0:T(8,128)} async-done(((f32[2,3,256,256]{3,2,1,0:T(8,128)}), f32[2,3,256,256]{3,2,1,0:T(8,128)}) %all-reduce.2.cloned.1.call-update) | async-done | bytes 1572880 | tf_op jit(solution)/shard_map/psum | solution.py:119
  647.8 3.2 multiply_subtract_fusion.3
  652.8 3.2 fusion.68
  (102 shorter events, 63.0 us)
Async XLA Ops:
  7.2 22.8 %copy-start.5 = (s32[1,1,8,2]{2,3,1,0:T(2,128)S(1)}, s32[1,1,8,2]{2,3,1,0:T(2,128)}, u32[]{:S(2)}) copy-start(s32[1,1,8,2]{2,3,1,0:T(2,128)} %param.18) | copy-start | bytes 196
  7.2 22.9 %copy-start.4 = (f32[2,3,256,256]{3,2,1,0:T(8,128)S(1)}, f32[2,3,256,256]{3,2,1,0:T(8,128)}, u32[]{:S(2)}) copy-start(f32[2,3,256,256]{3,2,1,0:T(8,128)} %param.16) | copy-start | bytes 4718596
  7.2 640.6 %all-reduce.2.cloned.1.call-start = ((), (), s32[]{:S(2)}) async-start(), calls=%async_computation | async-start | bytes 3145728 | tf_op jit(solution)/shard_map/psum | solution.py:119
  8.4 7.8 %collective-permute-start = (f32[2,128,256]{2,1,0:T(8,128)S(1)}, f32[2,128,256]{2,1,0:T(8,128)S(1)}, u32[]{:S(2)}, u32[]{:S(2)}) collective-permute-start(f32[2,128,256]{2,1,0:T(8,128)S(1)} %get-tuple-element.188), channel_id=1, source_target_pairs={{0,16},{16,32},{32,48},{48,64},{64,80},{80,96},{96,112},{1,17},{17... | collective-permute-start | bytes 786440 | tf_op jit(solution)/shard_map/ppermute | solution.py:22
  12.9 7.7 %collective-permute-start.1 = (f32[2,128,256]{2,1,0:T(8,128)S(1)}, f32[2,128,256]{2,1,0:T(8,128)S(1)}, u32[]{:S(2)}, u32[]{:S(2)}) collective-permute-start(f32[2,128,256]{2,1,0:T(8,128)S(1)} %get-tuple-element.187), channel_id=1, source_target_pairs={{16,0},{32,16},{48,32},{64,48},{80,64},{96,80},{112,96},{17,1},{33... | collective-permute-start | bytes 786440 | tf_op jit(solution)/shard_map/ppermute | solution.py:23
  20.6 1.5 copy-start.2
  23.8 28.3 %collective-permute-start.2 = (f32[2,1280,128]{2,1,0:T(8,128)}, f32[2,1280,128]{2,1,0:T(8,128)}, u32[]{:S(2)}, u32[]{:S(2)}) collective-permute-start(f32[2,1280,128]{2,1,0:T(8,128)} %get-tuple-element.185), channel_id=1, source_target_pairs={{0,1},{1,2},{2,3},{3,4},{4,5},{5,6},{6,7},{7,8},{8,9},{9,10},{10,1... | collective-permute-start | bytes 3932168 | tf_op jit(solution)/shard_map/ppermute | solution.py:22
  28.0 29.2 %collective-permute-start.3 = (f32[2,1280,128]{2,1,0:T(8,128)}, f32[2,1280,128]{2,1,0:T(8,128)}, u32[]{:S(2)}, u32[]{:S(2)}) collective-permute-start(f32[2,1280,128]{2,1,0:T(8,128)} %get-tuple-element.186), channel_id=1, source_target_pairs={{1,0},{2,1},{3,2},{4,3},{5,4},{6,5},{7,6},{8,7},{9,8},{10,9},{11,1... | collective-permute-start | bytes 3932168 | tf_op jit(solution)/shard_map/ppermute | solution.py:23
  160.6 14.1 %copy-start.1 = (f32[8,3,256,256]{3,2,1,0:T(8,128)}, f32[8,3,256,256]{3,2,1,0:T(8,128)S(1)}, u32[]{:S(2)}) copy-start(f32[8,3,256,256]{3,2,1,0:T(8,128)S(1)} %fusion.17) | copy-start | bytes 18874372
  209.4 16.2 %slice-start = ((s8[6291456]{0:T(1024)(128)(4,1)}), s8[4194304]{0:T(1024)(128)(4,1)S(1)}, s32[]{:S(2)}) async-start(s8[6291456]{0:T(1024)(128)(4,1)} %bitcast.122), calls=%async_computation.1 | async-start | bytes 8388608
  211.6 14.0 %slice-start.1 = ((s8[6291456]{0:T(1024)(128)(4,1)}), s8[2097152]{0:T(1024)(128)(4,1)S(1)}, s32[]{:S(2)}) async-start(s8[6291456]{0:T(1024)(128)(4,1)} %bitcast.122), calls=%async_computation.2 | async-start | bytes 4194304
  239.9 24.9 %slice-start.4 = ((s8[6291456]{0:T(1024)(128)(4,1)}), s8[2097152]{0:T(1024)(128)(4,1)S(1)}, s32[]{:S(2)}) async-start(s8[6291456]{0:T(1024)(128)(4,1)} %bitcast.126), calls=%async_computation.5 | async-start | bytes 4194304
  250.8 44.3 %copy-start = (f32[8,3,256,256]{3,2,1,0:T(8,128)}, f32[8,3,256,256]{3,2,1,0:T(8,128)S(1)}, u32[]{:S(2)}) copy-start(f32[8,3,256,256]{3,2,1,0:T(8,128)S(1)} %fusion.22) | copy-start | bytes 18874372
  250.8 13.9 %slice-start.5 = ((s8[6291456]{0:T(1024)(128)(4,1)}), s8[4194304]{0:T(1024)(128)(4,1)S(1)}, s32[]{:S(2)}) async-start(s8[6291456]{0:T(1024)(128)(4,1)} %bitcast.126), calls=%async_computation.6 | async-start | bytes 8388608
  250.8 30.0 %slice-start.6 = ((s8[6291456]{0:T(1024)(128)(4,1)}), s8[2097152]{0:T(1024)(128)(4,1)S(1)}, s32[]{:S(2)}) async-start(s8[6291456]{0:T(1024)(128)(4,1)} %bitcast.128), calls=%async_computation.7 | async-start | bytes 4194304
  264.7 16.1 %slice-start.7 = ((s8[6291456]{0:T(1024)(128)(4,1)}), s8[4194304]{0:T(1024)(128)(4,1)S(1)}, s32[]{:S(2)}) async-start(s8[6291456]{0:T(1024)(128)(4,1)} %bitcast.128), calls=%async_computation.8 | async-start | bytes 8388608
  264.7 30.4 %slice-start.2 = ((s8[6291456]{0:T(1024)(128)(4,1)}), s8[4194304]{0:T(1024)(128)(4,1)S(1)}, s32[]{:S(2)}) async-start(s8[6291456]{0:T(1024)(128)(4,1)} %bitcast.124), calls=%async_computation.3 | async-start | bytes 8388608
  280.9 14.3 %slice-start.3 = ((s8[6291456]{0:T(1024)(128)(4,1)}), s8[2097152]{0:T(1024)(128)(4,1)S(1)}, s32[]{:S(2)}) async-start(s8[6291456]{0:T(1024)(128)(4,1)} %bitcast.124), calls=%async_computation.4 | async-start | bytes 4194304
  448.8 29.1 %collective-permute-start.4 = (f32[2,1280,128]{2,1,0:T(8,128)S(1)}, f32[2,1280,128]{2,1,0:T(8,128)S(1)}, u32[]{:S(2)}, u32[]{:S(2)}) collective-permute-start(f32[2,1280,128]{2,1,0:T(8,128)S(1)} %slice.162), channel_id=1, source_target_pairs={{1,0},{2,1},{3,2},{4,3},{5,4},{6,5},{7,6},{8,7},{9,8},{10,9},{11,1... | collective-permute-start | bytes 3932168 | tf_op jit(solution)/shard_map/ppermute | solution.py:12
  481.6 29.3 %collective-permute-start.5 = (f32[2,1280,128]{2,1,0:T(8,128)}, f32[2,1280,128]{2,1,0:T(8,128)}, u32[]{:S(2)}, u32[]{:S(2)}) collective-permute-start(f32[2,1280,128]{2,1,0:T(8,128)} %get-tuple-element.181), channel_id=1, source_target_pairs={{0,1},{1,2},{2,3},{3,4},{4,5},{5,6},{6,7},{7,8},{8,9},{9,10},{10,1... | collective-permute-start | bytes 3932168 | tf_op jit(solution)/shard_map/ppermute | solution.py:12
  486.1 166.7 %copy-start.3 = (f32[2,1024,256]{2,1,0:T(8,128)S(1)}, f32[2,1024,256]{2,1,0:T(8,128)}, u32[]{:S(2)}) copy-start(f32[2,1024,256]{2,1,0:T(8,128)} %param.15) | copy-start | bytes 6291460
  514.9 17.4 %collective-permute-start.6 = (f32[2,128,256]{2,1,0:T(8,128)S(1)}, f32[2,128,256]{2,1,0:T(8,128)S(1)}, u32[]{:S(2)}, u32[]{:S(2)}) collective-permute-start(f32[2,128,256]{2,1,0:T(8,128)S(1)} %slice.189), channel_id=1, source_target_pairs={{16,0},{32,16},{48,32},{64,48},{80,64},{96,80},{112,96},{17,1},{33... | collective-permute-start | bytes 786440 | tf_op jit(solution)/shard_map/ppermute | solution.py:12
  534.0 117.0 %collective-permute-start.7 = (f32[2,128,256]{2,1,0:T(8,128)S(1)}, f32[2,128,256]{2,1,0:T(8,128)S(1)}, u32[]{:S(2)}, u32[]{:S(2)}) collective-permute-start(f32[2,128,256]{2,1,0:T(8,128)S(1)} %get-tuple-element.179), channel_id=1, source_target_pairs={{0,16},{16,32},{32,48},{48,64},{64,80},{80,96},{96,112},{1,17},{17... | collective-permute-start | bytes 786440 | tf_op jit(solution)/shard_map/ppermute | solution.py:12
Sparse Core Ops, SparseCore 0:
  486.2 161.5 all-reduce.1
where the time goes:
time: 676 us; the launch traced here: 663 us
  matrix products  234 us (35%)
  waiting for transfers between devices  211 us (31%)
  local copies, waits for them, and re-layouts  109 us (16%)
  other arithmetic  42.3 us (6%)
  loops' own time  31.2 us (5%)
  starting transfers between devices  20.4 us (3%)
  between operations  15.2 us (2%)
    psum x1, waiting for transfers between devices, on_device(): total = lax.psum(local_probe, ('row', 'col'))  112 us
    ppermute x4, waiting for transfers between devices, passed_along(): return lax.ppermute(block, axis, route)  68.1 us
    dynamic_update_slice x8, local copies, waits for them, and re-layouts, deposit(): return lax.dynamic_update_slice(total, current + patch_grads[slot], start)  52.9 us
    dot_general x2, matrix products, transform(): jnp.einsum('cmkn,nj->cmkj', left_real, sine, precision=highest)  41.9 us
    gather x24, local copies, waits for them, and re-layouts  32.5 us
    dot_general x2, matrix products, transform(): jnp.einsum('cmkn,nj->cmkj', left_real, cosine, precision=highest)  31.8 us
    another operation x1, loops' own time, on_device(): gradient = lax.fori_loop(0, capacity, deposit, jnp.zeros_like(padded))  31.1 us
    dot_general x2, matrix products, transform(): jnp.einsum('cmkn,nj->cmkj', left_imag, cosine, precision=highest)  30 us
  transfers between devices with their start and end apart: 9, of which 8 were waited for; matrix products, arithmetic and copies ran while one was open for 2% of the time, Pallas kernels for 0%

commit v1 on v0

v1 whole, which is shorter than its diff:
```python
import math

import jax
import jax.numpy as jnp
import ml_dtypes
import numpy as np
from jax import lax
from jax.experimental import pallas as pl
from jax.experimental.pallas import tpu as pltpu
from jax.sharding import PartitionSpec as P

N = 256
H = 128
MODES = 3
PAD_R = 1280
OBJ_R = 8192
OBJ_C = 4096


def tables():
    n = np.arange(H)[:, None]
    k = np.arange(H)[None, :]
    out = []
    for odd in (0, 1):
        angle = 2.0 * np.pi * ((n * (2 * k + odd)) % N) / N
        c, s = np.cos(angle) / 16.0, np.sin(angle) / 16.0
        full = np.block([[c, -s], [s, c]])
        for matrix in (full, full.T):
            high = matrix.astype(ml_dtypes.bfloat16)
            low = (matrix - high.astype(np.float64)).astype(ml_dtypes.bfloat16)
            out += [high, low]
    return np.stack(out)


def spread_table():
    matrix = np.zeros((N, N), np.float32)
    matrix[np.arange(0, N, 2), np.arange(H)] = 1.0
    matrix[np.arange(1, N, 2), np.arange(H) + H] = 1.0
    return matrix.astype(ml_dtypes.bfloat16)


def split(x):
    high = x.astype(jnp.bfloat16)
    return high, (x - high.astype(jnp.float32)).astype(jnp.bfloat16)


def mm(a, b):
    return jnp.dot(a, b, preferred_element_type=jnp.float32)


def by_right(x, high, low):
    xh, xl = split(x)
    return mm(jnp.concatenate([xh, xl, xh], axis=1), jnp.concatenate([high, high, low], axis=0))


def by_left(high, low, x):
    xh, xl = split(x)
    return mm(jnp.concatenate([high, low, high], axis=1), jnp.concatenate([xh, xh, xl], axis=0))


def rows_up(v, shift, row8):
    t = pltpu.roll(v.reshape(N // 8 + 1, 8, N), (8 - shift) % 8, 1)
    return jnp.where(row8 < 8 - shift, t[:-1], t[1:]).reshape(N, N)


def rows_down(v, shift, row8):
    t = pltpu.roll(v.reshape(N // 8, 8, N), shift, 1)
    none = jnp.zeros((1, 8, N), jnp.float32)
    return jnp.where(
        row8 >= shift, jnp.concatenate([t, none], axis=0), jnp.concatenate([none, t], axis=0)
    ).reshape(N + 8, N)


def body(off_ref, cnt_ref, base_ref, pad_ref, probe_ref, amp_ref, tab_ref, spread_ref, g_ref, pg_ref, spec_ref, half_ref):
    g_ref[...] = jnp.zeros_like(g_ref)
    pg_ref[...] = jnp.zeros_like(pg_ref)
    lane = lax.broadcasted_iota(jnp.int32, (N, N), 1)
    sub = lax.broadcasted_iota(jnp.int32, (N, N), 0)

    def visit(s, carry):
        y = off_ref[2 * s]
        x = off_ref[2 * s + 1]
        top = y - base_ref[0] + H
        left = x - base_ref[1] + H
        first = lane >= left
        first_tall = lax.broadcasted_iota(jnp.int32, (N + 8, N), 1) >= left
        row = sub + y
        ok_first = (lane + (base_ref[1] - H) >= 0) & first
        ok_second = (lane + (base_ref[1] + H) < OBJ_C) & (lane < left)
        row_ok = (row >= 0) & (row < OBJ_R)
        shift = top % 8
        low = pl.multiple_of(top - shift, 8)
        tall = pl.ds(low, N + 8)
        row8 = lax.broadcasted_iota(jnp.int32, (1, 8, N), 1)
        parts = []
        for c in range(2):
            a = rows_up(pad_ref[c, tall, 0:N], shift, row8)
            b = rows_up(pad_ref[c, tall, N : 2 * N], shift, row8)
            v = jnp.where(ok_first & row_ok, a, jnp.where(ok_second & row_ok, b, 0.0))
            parts.append(pltpu.roll(v, (N - left) % N, 1))
        pr, pi = parts

        spread = spread_ref[...]
        half_ref[0] = amp_ref[s, :, 0:H]
        half_ref[1] = amp_ref[s, :, H:N]
        amp = jnp.concatenate(
            [jnp.concatenate([half_ref[i, pl.ds(o, H, 2), :] for i in range(2)], axis=1) for o in range(2)], axis=0
        )
        ah, al = split(amp)
        amp = mm(jnp.concatenate([ah, al], axis=1), jnp.concatenate([spread, spread], axis=0))

        power = [0.0, 0.0]
        for m in range(MODES):
            qr, qi = probe_ref[0, m], probe_ref[1, m]
            wr = qr * pr - qi * pi
            wi = qr * pi + qi * pr
            a = jnp.concatenate([wr[:, :H] + wr[:, H:], wi[:, :H] + wi[:, H:]], axis=1)
            b = jnp.concatenate([wr[:, :H] - wr[:, H:], wi[:, :H] - wi[:, H:]], axis=1)
            ye = by_right(a, tab_ref[0], tab_ref[1])
            yo = by_right(b, tab_ref[4], tab_ref[5])
            se, so = ye[:H] + ye[H:], yo[:H] + yo[H:]
            de, do = ye[:H] - ye[H:], yo[:H] - yo[H:]

            def stack(e, o):
                return jnp.concatenate(
                    [jnp.concatenate([e[:, :H], o[:, :H]], axis=1), jnp.concatenate([e[:, H:], o[:, H:]], axis=1)], axis=0
                )

            ze = by_left(tab_ref[2], tab_ref[3], stack(se, so))
            zo = by_left(tab_ref[6], tab_ref[7], stack(de, do))
            spec_ref[m, 0] = ze
            spec_ref[m, 1] = zo
            for i, z in enumerate((ze, zo)):
                power[i] = power[i] + (z[:H] * z[:H] + z[H:] * z[H:])
        ratios = [1.0 - amp[i * H : (i + 1) * H] * lax.rsqrt(jnp.maximum(power[i], 1.0)) for i in range(2)]
        ratios = [jnp.concatenate([r, r], axis=0) for r in ratios]
        gr, gi = 0.0, 0.0
        for m in range(MODES):
            e = by_left(tab_ref[0], tab_ref[1], spec_ref[m, 0] * ratios[0])
            o = by_left(tab_ref[4], tab_ref[5], spec_ref[m, 1] * ratios[1])
            lo, hi = e + o, e - o

            def lanes(k):
                k = slice(k * H, (k + 1) * H)
                return jnp.concatenate(
                    [jnp.concatenate([lo[:H, k], lo[H:, k]], axis=1), jnp.concatenate([hi[:H, k], hi[H:, k]], axis=1)], axis=0
                )

            e = by_right(lanes(0), tab_ref[2], tab_ref[3])
            o = by_right(lanes(1), tab_ref[6], tab_ref[7])
            lo, hi = e + o, e - o
            cr = jnp.concatenate([lo[:, :H], hi[:, :H]], axis=1)
            ci = jnp.concatenate([lo[:, H:], hi[:, H:]], axis=1)
            qr, qi = probe_ref[0, m], probe_ref[1, m]
            gr = gr + (qr * cr + qi * ci)
            gi = gi + (qr * ci - qi * cr)
            pg_ref[0, m] += pr * cr + pi * ci
            pg_ref[1, m] += pr * ci - pi * cr
        for c, g in enumerate((gr, gi)):
            v = rows_down(pltpu.roll(g, left, 1), shift, row8)
            g_ref[c, tall, 0:N] += jnp.where(first_tall, v, 0.0)
            g_ref[c, tall, N : 2 * N] += jnp.where(first_tall, 0.0, v)
        return carry

    lax.fori_loop(0, cnt_ref[0], visit, 0)


def local_step(padded, probe, amp, offsets, count, base):
    vm = pl.BlockSpec(memory_space=pltpu.VMEM)
    sm = pl.BlockSpec(memory_space=pltpu.SMEM)
    return pl.pallas_call(
        body,
        out_shape=(
            jax.ShapeDtypeStruct((2, PAD_R, 2 * N), jnp.float32),
            jax.ShapeDtypeStruct((2, MODES, N, N), jnp.float32),
        ),
        in_specs=[sm, sm, sm, vm, vm, vm, vm, vm],
        out_specs=(vm, vm),
        scratch_shapes=[pltpu.VMEM((MODES, 2, N, N), jnp.float32), pltpu.VMEM((2, N, H), jnp.float32)],
        compiler_params=pltpu.CompilerParams(vmem_limit_bytes=56 * 2**20),
        name="windows",
    )(offsets, count, base, padded, probe, amp, jnp.asarray(tables()), jnp.asarray(spread_table()))


MESH = pl.DeviceIdType.MESH
T = 1024
F32 = jnp.float32
ROWS, COLS = 8, 16
PR = 1536


def push(src, dst, sems, i, where):
    c = pltpu.make_async_remote_copy(
        src_ref=src, dst_ref=dst, send_sem=sems.at[0, i], recv_sem=sems.at[1, i], device_id=where, device_id_type=MESH
    )
    c.start()
    return c


def greet(peers):
    barrier = pltpu.get_barrier_semaphore()
    for p in peers:
        pl.semaphore_signal(barrier, inc=1, device_id=p, device_id_type=MESH)
    pl.semaphore_wait(barrier, len(peers))


def around():
    r, c = lax.axis_index("row"), lax.axis_index("col")
    up, down = ((r + ROWS - 1) % ROWS, c), ((r + 1) % ROWS, c)
    left, right = (r, (c + COLS - 1) % COLS), (r, (c + 1) % COLS)
    return r, c, up, down, left, right


def halo_body(obj, pad, own_sem, sems):
    r, c, up, down, left, right = around()
    greet((up, down, left, right))
    own = pltpu.make_async_copy(obj, pad.at[:, H : H + T, H : H + N], own_sem)
    copies = []
    for rows in ((0, H), (T - H, H), (H, T - N)):
        a, n = rows
        copies.append(push(obj.at[:, a : a + n, H:N], pad.at[:, H + a : H + a + n, 0:H], sems, len(copies), right))
        copies.append(push(obj.at[:, a : a + n, 0:H], pad.at[:, H + a : H + a + n, H + N :], sems, len(copies), left))
    copies.append(push(obj.at[:, T - H : T], pad.at[:, 0:H, H : H + N], sems, 6, down))
    copies.append(push(obj.at[:, 0:H], pad.at[:, H + T :, H : H + N], sems, 7, up))
    own.start()
    for k, lanes in ((0, slice(0, H)), (1, slice(H + N, 2 * N))):
        copies[k].wait_recv()
        copies.append(push(pad.at[:, H:N, lanes], pad.at[:, H + T :, lanes], sems, 8 + 2 * k, up))
        copies[2 + k].wait_recv()
        copies.append(push(pad.at[:, T : T + H, lanes], pad.at[:, 0:H, lanes], sems, 9 + 2 * k, down))
    own.wait()
    for i, copy in enumerate(copies):
        if i >= 4:
            copy.wait_recv()
    for copy in copies:
        copy.wait_send()


def halo(obj, space=pl.ANY):
    spec = pl.BlockSpec(memory_space=space)
    return pl.pallas_call(
        halo_body,
        out_shape=jax.ShapeDtypeStruct((2, PAD_R, 2 * N), F32),
        in_specs=[spec],
        out_specs=spec,
        scratch_shapes=[pltpu.SemaphoreType.DMA, pltpu.SemaphoreType.DMA((2, 12))],
        compiler_params=pltpu.CompilerParams(collective_id=1, has_side_effects=True, vmem_limit_bytes=40 * 2**20),
        name="halo",
    )(obj)


BIG, SMALL = 1024, 512


def finish_body(g, pg, obj, probe, out, newp, edge, from_rows, from_cols, half, acc, rb1, rs1, rb2, rs2, sems):
    r, c, up, down, left, right = around()
    x, core, z, y = r // 2, r % 2, c // 4, c % 4
    partner = (x * 2 + 1 - core, c)
    a, b = x + core * (z - x), z + core * (x - z)

    def dev(a_, b_, y_):
        return ((a_ + core * (b_ - a_)) * 2 + core, (b_ + core * (a_ - b_)) * 4 + y_)

    line_a = [dev((a + d) % 4, b, y) for d in range(1, 4)]
    line_b = [dev(a, (b + d) % 4, y) for d in range(1, 4)]
    by, ay = b * 4 + y, a * 4 + y
    plane_b = [dev(a, (by + d) % 16 // 4, (by + d) % 16 % 4) for d in range(1, 16)]
    plane_a = [dev((ay + d) % 16 // 4, b, (ay + d) % 16 % 4) for d in range(1, 16)]
    extra = [dev((a + d) % 4, b, (y + e) % 4) for d in range(1, 4) for e in range(4)]
    greet(plane_b + extra + [up, down])

    copies = []

    def go(src, dst, where):
        copies.append(push(src, dst, sems, len(copies), where))
        return copies[-1]

    mine = pl.ds(pl.multiple_of(core * H, H), H)
    other = pl.ds(pl.multiple_of((1 - core) * H, H), H)
    row_copies = [
        go(g.at[:, 0:H], from_rows.at[0], up),
        go(g.at[:, H + T :], from_rows.at[1], down),
    ]
    core_copy = go(pg.at[:, other], half, partner)
    col_copies = []

    def to_cols(src, lo, hi):
        col_copies.append(go(src.at[:, :, 0:H], from_cols.at[0, :, lo:hi], left))
        col_copies.append(go(src.at[:, :, H + N :], from_cols.at[1, :, lo:hi], right))

    to_cols(g.at[:, N:T], H, T - H)

    core_copy.wait_recv()
    acc[...] = pg[:, mine] + half[...]
    na, nb = BIG // 4, SMALL // 4
    first = []
    for d in range(1, 4):
        first.append(go(acc.at[pl.ds(pl.multiple_of((a + d) % 4 * na, na), na)], rb1.at[d - 1], line_a[d - 1]))
        first.append(go(acc.at[pl.ds(pl.multiple_of(BIG + (b + d) % 4 * nb, nb), nb)], rs1.at[d - 1], line_b[d - 1]))

    keep_above = (r > 0).astype(F32)
    keep_below = (r < ROWS - 1).astype(F32)
    row_copies[0].wait_recv()
    edge[0] = g[:, T : T + H] + from_rows[0] * keep_below
    row_copies[1].wait_recv()
    edge[1] = g[:, H:N] + from_rows[1] * keep_above
    to_cols(edge.at[0], T - H, T)
    to_cols(edge.at[1], 0, H)

    for copy in first:
        copy.wait_recv()
    ra = pl.multiple_of(a * na, na)
    rb = pl.multiple_of(BIG + b * nb, nb)
    acc[pl.ds(ra, na)] += rb1[0] + rb1[1] + rb1[2]
    acc[pl.ds(rb, nb)] += rs1[0] + rs1[1] + rs1[2]
    ma, mb = na // 16, nb // 16
    second = []
    for d in range(1, 16):
        second.append(go(acc.at[pl.ds(pl.multiple_of(ra + (by + d) % 16 * ma, ma), ma)], rb2.at[d - 1], plane_b[d - 1]))
        second.append(go(acc.at[pl.ds(pl.multiple_of(rb + (ay + d) % 16 * mb, mb), mb)], rs2.at[d - 1], plane_a[d - 1]))

    out[:, 0:H] = obj[:, 0:H] - 0.25 * edge[1, :, :, H : H + N]
    out[:, H : T - H] = obj[:, H : T - H] - 0.25 * g[:, N:T, H : H + N]
    out[:, T - H :] = obj[:, T - H :] - 0.25 * edge[0, :, :, H : H + N]

    for copy in second:
        copy.wait_recv()
    qa = pl.ds(pl.multiple_of(ra + by * ma, ma), ma)
    qb = pl.ds(pl.multiple_of(rb + ay * mb, mb), mb)
    factor = 0.5 / math.sqrt(1024.0)
    newp[qa, mine] = probe[qa, mine] - factor * (acc[qa] + jnp.sum(rb2[...], axis=0))
    newp[qb, mine] = probe[qb, mine] - factor * (acc[qb] + jnp.sum(rs2[...], axis=0))
    third = []
    for d in range(15):
        third.append(go(newp.at[qa, mine], newp.at[qa, mine], plane_b[d]))
        third.append(go(newp.at[qb, mine], newp.at[qb, mine], plane_a[d]))
    for copy in third:
        copy.wait_recv()
    fourth = []
    sa, sb = pl.ds(ra, na), pl.ds(rb, nb)
    for d in range(3):
        fourth.append(go(newp.at[sa, mine], newp.at[sa, mine], line_a[d]))
        fourth.append(go(newp.at[sb, mine], newp.at[sb, mine], line_b[d]))
    for copy in fourth:
        copy.wait_recv()
    last = go(newp.at[:, mine], newp.at[:, mine], partner)

    for copy in col_copies:
        copy.wait_recv()
    keep_left = (c > 0).astype(F32) * 0.25
    keep_right = (c < COLS - 1).astype(F32) * 0.25
    out[:, :, H:N] -= from_cols[0] * keep_right
    out[:, :, 0:H] -= from_cols[1] * keep_left
    last.wait_recv()
    for copy in copies:
        copy.wait_send()


def finish(g, pg, obj, probe):
    vm = pl.BlockSpec(memory_space=pltpu.VMEM)
    na, nb = BIG // 4, SMALL // 4
    out, newp = pl.pallas_call(
        finish_body,
        out_shape=(jax.ShapeDtypeStruct((2, T, N), F32), jax.ShapeDtypeStruct((PR, N), F32)),
        in_specs=[vm] * 4,
        out_specs=(vm, vm),
        scratch_shapes=[
            pltpu.VMEM((2, 2, H, 2 * N), F32),
            pltpu.VMEM((2, 2, H, 2 * N), F32),
            pltpu.VMEM((2, 2, T, H), F32),
            pltpu.VMEM((PR, H), F32),
            pltpu.VMEM((PR, H), F32),
            pltpu.VMEM((3, na, H), F32),
            pltpu.VMEM((3, nb, H), F32),
            pltpu.VMEM((15, na // 16, H), F32),
            pltpu.VMEM((15, nb // 16, H), F32),
            pltpu.SemaphoreType.DMA((2, 82)),
        ],
        compiler_params=pltpu.CompilerParams(collective_id=2, has_side_effects=True, vmem_limit_bytes=56 * 2**20),
        name="finish",
    )(g, pg.reshape(PR, N), obj, probe.reshape(PR, N))
    return out, newp.reshape(probe.shape)


def on_device(object_field, probe_modes, amplitudes, scan_offsets, slot_counts):
    base = jnp.stack([lax.axis_index("row") * T, lax.axis_index("col") * N]).astype(jnp.int32)
    padded = halo(object_field)
    g, pg = local_step(
        padded,
        probe_modes,
        amplitudes.reshape(8, N, N),
        scan_offsets.reshape(16),
        slot_counts.reshape(1),
        base,
    )
    return finish(g, pg, object_field, probe_modes)


def solution(mesh):
    placed = (
        P(None, "row", "col"),
        P(),
        P("row", "col", None, None, None),
        P("row", "col", None, None),
        P("row", "col"),
    )
    return jax.shard_map(
        on_device,
        mesh=mesh,
        in_specs=placed,
        out_specs=(P(None, "row", "col"), P()),
        check_vma=False,
    )
```

time: 676 us -> 146 us (0.22); the launches traced: 663 us -> 146 us
  matrix products: 234 us -> 0 us
  waiting for transfers between devices: 211 us -> 0 us
  Pallas kernels: 0 us -> 134 us
  local copies, waits for them, and re-layouts: 109 us -> 9.56 us
  other arithmetic: 42.3 us -> 0.59 us
  loops' own time: 31.2 us -> 0 us
  starting transfers between devices: 20.4 us -> 0 us
  between operations: 15.2 us -> 1.32 us
    dot_general x16 -> x0, matrix products: 234 us -> none  [the longest x2 41.9 us: transform(): jnp.einsum('cmkn,nj->cmkj', left_real, sine, precision=highest)]
    pallas_call x0 -> x3, Pallas kernels: none -> 134 us  [the longest x1 78 us: finish(): pl.pallas_call(finish_body, out_shape=(jax.ShapeDtypeStruct((2, T, N), F3...]
    psum x1 -> x0, waiting for transfers between devices: 112 us -> none  [on_device(): total = lax.psum(local_probe, ('row', 'col'))]
    ppermute x8 -> x0, waiting for transfers between devices: 99.1 us -> none  [the longest x4 68.1 us: passed_along(): return lax.ppermute(block, axis, route)]
    dynamic_update_slice x8 -> x0, local copies, waits for them, and re-layouts: 52.9 us -> none  [deposit(): return lax.dynamic_update_slice(total, current + patch_grads[slot], start)]
    gather x24 -> x0, local copies, waits for them, and re-layouts: 32.5 us -> none
    another operation x2 -> x0, loops' own time: 31.2 us -> none  [the longest x1 31.1 us: on_device(): gradient = lax.fori_loop(0, capacity, deposit, jnp.zeros_like(padded))]
    ppermute x8 -> x0, starting transfers between devices: 20.3 us -> none  [the longest x2 8.76 us: extended(): before = lax.ppermute(last, axis, up)]
  transfers between devices with their start and end apart: 9 -> 0, of which waited for: 8 -> 0; matrix products, arithmetic and copies ran while one was open for 2% -> 0% of each run, Pallas kernels for 0% -> 0%
where the time goes in v1:
time: 146 us
  Pallas kernels  134 us (92%)
  local copies, waits for them, and re-layouts  9.56 us (7%)
    pallas_call x1, Pallas kernels, finish(): pl.pallas_call(finish_body, out_shape=(jax.ShapeDtypeStruct((2, T, N), F3...  78 us
    pallas_call x1, Pallas kernels, halo(): pl.pallas_call(halo_body, out_shape=jax.ShapeDtypeStruct((2, PAD_R, 2 * N...  31.5 us
    pallas_call x1, Pallas kernels, local_step(): pl.pallas_call(body, out_shape=(jax.ShapeDtypeStruct((2, PAD_R, 2 * N), j...  24.8 us
    unnamed x9, local copies, waits for them, and re-layouts  8.97 us

profile of v1, /device:TPU:1, one launch (start us, length us, event | category | flops | bytes accessed | tf_op | source)
XLA Modules:
  0.0 145.7 jit_solution(16413815491607566735)
XLA Ops:
  1.3 0.6 pad_add_fusion.base_ref
  1.9 0.8 copy.10
  2.6 0.6 reshape.22.off_ref
  3.2 0.0 copy-start.1
  3.2 1.6 %copy-done.1 = f32[2,1024,256]{2,1,0:T(8,128)S(1)} copy-done((f32[2,1024,256]{2,1,0:T(8,128)S(1)}, f32[2,1024,256]{2,1,0:T(8,128)}, u32[]{:S(2)}) %copy-start.1) | copy-done | bytes 2097176
  4.8 31.5 %halo.1.pad_ref = f32[2,1280,512]{2,1,0:T(8,128)S(1)} custom-call(f32[2,1024,256]{2,1,0:T(8,128)S(1)} %copy-done.1), custom_call_target="tpu_custom_call" | custom-call | tf_op jit(solution)/shard_map/halo/pallas_call | solution.py:241
  36.3 0.0 copy-start
  36.3 2.3 %copy-done = f32[2,1280,512]{2,1,0:T(8,128)} copy-done((f32[2,1280,512]{2,1,0:T(8,128)}, f32[2,1280,512]{2,1,0:T(8,128)S(1)}, u32[]{:S(2)}) %copy-start) | copy-done | bytes 5242904
  38.6 24.8 %windows.1 = (f32[2,1280,512]{2,1,0:T(8,128)}, f32[2,3,256,256]{3,2,1,0:T(8,128)}) custom-call(s32[16]{0:T(128)} %reshape.22.off_ref, s32[1]{0:T(128)} %bitcast.9.cnt_ref, s32[2]{0:T(128)} %pad_add_fusion.base_ref, f32[2,1280,512]{2,1,0:T(8,128)} %copy-done, f32[2,3,256,256]{3,2,1,0:T(8,128)} %probe_ref.1, f32[8,256,256]{2,1,0:T(8,128)} %bitcast.11, ...), custom_call_target="tpu_custom_call" | custom-call | tf_op jit(solution)/shard_map/windows/pallas_call | solution.py:171
  63.4 78.0 %finish.1 = (f32[2,1024,256]{2,1,0:T(8,128)}, f32[1536,256]{1,0:T(8,128)}) custom-call(f32[2,1280,512]{2,1,0:T(8,128)} %get-tuple-element.6.g, f32[1536,256]{1,0:T(8,128)} %bitcast.12, f32[2,1024,256]{2,1,0:T(8,128)} %obj.3, f32[1536,256]{1,0:T(8,128)} %bitcast.10), custom_call_target="tpu_custom_call" | custom-call | tf_op jit(solution)/shard_map/finish/pallas_call | solution.py:362
  141.4 0.0 copy-start.2
  141.4 3.2 %copy.14 = f32[2,1024,256]{2,1,0:T(8,128)} copy(f32[2,1024,256]{2,1,0:T(8,128)} %get-tuple-element.12) | data formatting | bytes 4194304
  144.6 0.0 copy-done.2
  144.6 1.1 copy.15
Async XLA Ops:
  3.2 1.6 %copy-start.1 = (f32[2,1024,256]{2,1,0:T(8,128)S(1)}, f32[2,1024,256]{2,1,0:T(8,128)}, u32[]{:S(2)}) copy-start(f32[2,1024,256]{2,1,0:T(8,128)} %obj.3) | copy-start | bytes 6291460
  36.3 2.3 %copy-start = (f32[2,1280,512]{2,1,0:T(8,128)}, f32[2,1280,512]{2,1,0:T(8,128)S(1)}, u32[]{:S(2)}) copy-start(f32[2,1280,512]{2,1,0:T(8,128)S(1)} %halo.1.pad_ref) | copy-start | bytes 15728644
  141.4 3.2 %copy-start.2 = (f32[1536,256]{1,0:T(8,128)S(1)}, f32[1536,256]{1,0:T(8,128)}, u32[]{:S(2)}) copy-start(f32[1536,256]{1,0:T(8,128)} %get-tuple-element.9) | copy-start | bytes 4718596

commit v2 on v0

v2 whole, which is shorter than its diff:
```python
import math

import jax
import jax.numpy as jnp
import ml_dtypes
import numpy as np
from jax import lax
from jax.experimental import pallas as pl
from jax.experimental.pallas import tpu as pltpu
from jax.sharding import PartitionSpec as P

N = 256
H = 128
MODES = 3
PAD_R = 1280
T = 1024
SLOTS = 8
ROWS, COLS = 8, 16
MESH = pl.DeviceIdType.MESH
F32 = jnp.float32
BF16 = jnp.bfloat16
OBJ_R = 8192
OBJ_C = 4096


def tables():
    n = np.arange(H)[:, None]
    k = np.arange(H)[None, :]
    out = []
    for odd in (0, 1):
        angle = 2.0 * np.pi * ((n * (2 * k + odd)) % N) / N
        c, s = np.cos(angle) / 16.0, np.sin(angle) / 16.0
        full = np.block([[c, -s], [s, c]])
        for matrix in (full, full.T):
            high = matrix.astype(ml_dtypes.bfloat16)
            low = (matrix - high.astype(np.float64)).astype(ml_dtypes.bfloat16)
            out += [high, low]
    return np.stack(out)


def spread_table():
    matrix = np.zeros((N, N), np.float32)
    matrix[np.arange(0, N, 2), np.arange(H)] = 1.0
    matrix[np.arange(1, N, 2), np.arange(H) + H] = 1.0
    return matrix.astype(ml_dtypes.bfloat16)


def split(x):
    high = x.astype(BF16)
    return high, (x - high.astype(F32)).astype(BF16)


def right(pair, high, low):
    xh, xl = pair
    return jnp.dot(
        jnp.concatenate([xh, xl, xh], axis=1), jnp.concatenate([high, high, low], axis=0), preferred_element_type=F32
    )


def left(high, low, pair):
    xh, xl = pair
    return jnp.dot(
        jnp.concatenate([high, low, high], axis=1), jnp.concatenate([xh, xh, xl], axis=0), preferred_element_type=F32
    )


def beside(a, b):
    return jnp.concatenate([a, b], axis=1)


def above(a, b):
    return jnp.concatenate([a, b], axis=0)


def rows_up(tiles, shift, back, row8):
    t = [pltpu.roll(v, back, 0) for v in tiles]
    return jnp.concatenate([jnp.where(row8 < 8 - shift, p, q) for p, q in zip(t[:-1], t[1:])], axis=0)


def rows_down(v, shift, row8):
    t = pltpu.roll(v.reshape(N // 8, 8, N), shift, 1)
    none = jnp.zeros((1, 8, N), F32)
    return jnp.where(row8[None] >= shift, jnp.concatenate([t, none], axis=0), jnp.concatenate([none, t], axis=0))


GEO = 32
FIRST, SHIFT, LEFT, BACK_ROW, BACK_COL, ROW, PLACES = range(7)
HT, TT, PT = H // 8, T // 8, PAD_R // 8
TALL = 2 * HT + N // 8 + 1


def geometry(scan_offsets):
    off = scan_offsets.reshape(SLOTS, 2)
    top, lft = (off[:, 0] + H) % T, (off[:, 1] + H) % N
    shift = top % 8
    first = top // 8
    places = jnp.clip(jnp.arange(0, PT, 8)[None] - first[:, None] + HT, 0, TALL - 8)
    fixed = jnp.stack([first, shift, lft, (8 - shift) % 8, (N - lft) % N, off[:, 0]], axis=1)
    table = jnp.concatenate([fixed, places], axis=1).astype(jnp.int32)
    return jnp.pad(table, ((0, 0), (0, GEO - table.shape[1]))).reshape(SLOTS * GEO)


def body(
    geo, cnt, obj, probe_hbm, amp_hbm, tab_hbm, spread_hbm,
    out, newp,
    pad, probe, amp, tab, spread, halves, spec, sh, sl, patch, tall, from_rows, from_cols,
    pg, half, acc, rb1, rb2, local, sems,
):
    r, c = lax.axis_index("row"), lax.axis_index("col")
    up, down = ((r + ROWS - 1) % ROWS, c), ((r + 1) % ROWS, c)
    west, east = (r, (c + COLS - 1) % COLS), (r, (c + 1) % COLS)
    x, core, z, y = r // 2, r % 2, c // 4, c % 4
    partner = (x * 2 + 1 - core, c)
    a, b = x + core * (z - x), z + core * (x - z)

    def dev(a_, b_, y_):
        return ((a_ + core * (b_ - a_)) * 2 + core, (b_ + core * (a_ - b_)) * 4 + y_)

    by = b * 4 + y
    line = [dev((a + d) % 4, b, y) for d in range(1, 4)]
    plane = [dev(a, (by + d) % 16 // 4, (by + d) % 16 % 4) for d in range(1, 16)]

    fetch = [
        pltpu.make_async_copy(src, dst, local.at[i])
        for i, (src, dst) in enumerate(
            (
                (obj, pad.at[:, HT : HT + TT, :, H : H + N]),
                (amp_hbm, amp),
                (spread_hbm, spread),
                (probe_hbm, probe),
                (tab_hbm, tab),
                (obj, out),
            )
        )
    ]
    for f in fetch:
        f.start()

    peers = plane + line + [up, down, west, east]
    barrier = pltpu.get_barrier_semaphore()
    for p in peers:
        pl.semaphore_signal(barrier, inc=1, device_id=p, device_id_type=MESH)
    pl.semaphore_wait(barrier, len(peers))

    count, copies_out = [0], []

    def go(src, dst, where):
        i = count[0]
        count[0] += 1
        copy = pltpu.make_async_remote_copy(
            src_ref=src, dst_ref=dst, send_sem=sems.at[0, i], recv_sem=sems.at[1, i], device_id=where, device_id_type=MESH
        )
        copy.start()
        copies_out.append(copy)
        return copy

    cols = []
    for lo, hi in ((0, HT), (TT - HT, TT), (HT, TT - HT)):
        cols.append(go(obj.at[:, lo:hi, :, H:N], pad.at[:, HT + lo : HT + hi, :, 0:H], east))
        cols.append(go(obj.at[:, lo:hi, :, 0:H], pad.at[:, HT + lo : HT + hi, :, H + N :], west))
    rows = [
        go(obj.at[:, TT - HT : TT], pad.at[:, 0:HT, :, H : H + N], down),
        go(obj.at[:, 0:HT], pad.at[:, HT + TT :, :, H : H + N], up),
    ]
    for k, lanes in ((0, slice(0, H)), (1, slice(H + N, 2 * N))):
        cols[k].wait_recv()
        rows.append(go(pad.at[:, HT : 2 * HT, :, lanes], pad.at[:, HT + TT :, :, lanes], up))
        cols[2 + k].wait_recv()
        rows.append(go(pad.at[:, TT : TT + HT, :, lanes], pad.at[:, 0:HT, :, lanes], down))

    fetch[1].wait()
    fetch[2].wait()

    def order(s, carry):
        halves[0] = amp[s, :, 0:H]
        halves[1] = amp[s, :, H:N]
        v = above(*(beside(*(halves[i, pl.ds(o, H, 2), :] for i in range(2))) for o in range(2)))
        vh, vl = split(v)
        amp[s] = jnp.dot(beside(vh, vl), above(spread[...], spread[...]), preferred_element_type=F32)
        tall[s, :, 0:HT] = jnp.zeros((2, HT, 8, N), F32)
        tall[s, :, TALL - HT :] = jnp.zeros((2, HT, 8, N), F32)
        return carry

    lax.fori_loop(0, SLOTS, order, 0)
    for f in (fetch[0], fetch[3], fetch[4], fetch[5]):
        f.wait()
    for copy in rows + cols[4:]:
        copy.wait_recv()
    for copy in rows + cols:
        copy.wait_send()
    del copies_out[:]

    lane = lax.broadcasted_iota(jnp.int32, (N, N), 1)
    sub = lax.broadcasted_iota(jnp.int32, (N, N), 0)
    row8 = lax.broadcasted_iota(jnp.int32, (8, N), 0)
    col0 = c * N - H

    def forward(s, carry):
        g = s * GEO
        first, shift, lft = geo[g + FIRST], geo[g + SHIFT], geo[g + LEFT]
        row = sub + geo[g + ROW]
        row_ok = (row >= 0) & (row < OBJ_R)
        ok_first = row_ok & (lane >= lft) & (lane + col0 >= 0)
        ok_second = row_ok & (lane < lft) & (lane + (col0 + N) < OBJ_C)
        for i in range(2):
            sides = []
            for lanes in (slice(0, N), slice(N, 2 * N)):
                tiles = [pad[i, first + k, :, lanes] for k in range(N // 8 + 1)]
                sides.append(rows_up(tiles, shift, geo[g + BACK_ROW], row8))
            v = jnp.where(ok_first, sides[0], jnp.where(ok_second, sides[1], 0.0))
            patch[s, i] = pltpu.roll(v, geo[g + BACK_COL], 1)
        pr, pi = patch[s, 0], patch[s, 1]
        plus, minus = [], []
        for m in range(MODES):
            qr, qi = probe[0, m], probe[1, m]
            wr = qr * pr - qi * pi
            wi = qr * pi + qi * pr
            plus.append(beside(wr[:, :H] + wr[:, H:], wi[:, :H] + wi[:, H:]))
            minus.append(beside(wr[:, :H] - wr[:, H:], wi[:, :H] - wi[:, H:]))
        ye = right(split(jnp.concatenate(plus, axis=0)), tab[0], tab[1])
        yo = right(split(jnp.concatenate(minus, axis=0)), tab[4], tab[5])
        power = [0.0, 0.0]
        for m in range(MODES):
            k = m * N
            parts = []
            for sign in (1.0, -1.0):
                e = ye[k : k + H] + sign * ye[k + H : k + N]
                o = yo[k : k + H] + sign * yo[k + H : k + N]
                parts.append(above(beside(e[:, :H], o[:, :H]), beside(e[:, H:], o[:, H:])))
            for i, part in enumerate(parts):
                v = left(tab[2 + 4 * i], tab[3 + 4 * i], split(part))
                spec[m, i] = v
                power[i] = power[i] + (v[:H] * v[:H] + v[H:] * v[H:])
        live = jnp.where(jnp.zeros((1, N), jnp.int32) + s < cnt[0, 0], 1.0, 0.0)
        for i in range(2):
            ratio = live * (1.0 - amp[s, i * H : (i + 1) * H] * lax.rsqrt(jnp.maximum(power[i], 1.0)))
            ratio = above(ratio, ratio)
            for m in range(MODES):
                vh, vl = split(spec[m, i] * ratio)
                sh[(s * MODES + m) * 2 + i] = vh
                sl[(s * MODES + m) * 2 + i] = vl
        return carry

    lax.fori_loop(0, SLOTS, forward, 0)

    def inverse(m, slots):
        even, odd = [], []
        for s in slots:
            k = (s * MODES + m) * 2
            e = left(tab[0], tab[1], (sh[k], sl[k]))
            o = left(tab[4], tab[5], (sh[k + 1], sl[k + 1]))
            lo, hi = e + o, e - o
            even += [beside(lo[:H, :H], lo[H:, :H]), beside(hi[:H, :H], hi[H:, :H])]
            odd += [beside(lo[:H, H:], lo[H:, H:]), beside(hi[:H, H:], hi[H:, H:])]
        e = right(split(jnp.concatenate(even, axis=0)), tab[2], tab[3])
        o = right(split(jnp.concatenate(odd, axis=0)), tab[6], tab[7])
        qr, qi = probe[0, m], probe[1, m]
        mode_r, mode_i = 0.0, 0.0
        for i, s in enumerate(slots):
            ee, oo = e[i * N : (i + 1) * N], o[i * N : (i + 1) * N]
            lo, hi = ee + oo, ee - oo
            cr = beside(lo[:, :H], hi[:, :H])
            ci = beside(lo[:, H:], hi[:, H:])
            pr, pi = patch[s, 0], patch[s, 1]
            mode_r = mode_r + (pr * cr + pi * ci)
            mode_i = mode_i + (pr * ci - pi * cr)
            grads = (qr * cr + qi * ci, qr * ci - qi * cr)
            for k, g in enumerate(grads):
                inner = slice(HT, HT + N // 8)
                if m > 0:
                    g = g + tall[s, k, inner].reshape(N, N)
                if m < MODES - 1:
                    tall[s, k, inner] = g.reshape(N // 8, 8, N)
                else:
                    g = pltpu.roll(g, geo[s * GEO + LEFT], 1)
                    tall[s, k, HT : TALL - HT] = rows_down(g, geo[s * GEO + SHIFT], row8)
        pg[m, 0:N] += mode_r
        pg[m, N:] += mode_i

    mine = pl.ds(pl.multiple_of(core * H, H), H)
    other = pl.ds(pl.multiple_of((1 - core) * H, H), H)
    factor = 0.5 / math.sqrt(ROWS * COLS * SLOTS)

    def probe_sum(m):
        copy = go(pg.at[m, :, other], half.at[m], partner)
        yield
        copy.wait_recv()
        acc[m] = pg[m, :, mine] + half[m]
        sent = []
        for d in range(1, 4):
            piece = pl.ds(pl.multiple_of((a + d) % 4 * H, H), H)
            sent.append(go(acc.at[m, piece], rb1.at[m, d - 1], line[d - 1]))
        yield
        for copy in sent:
            copy.wait_recv()
        start = pl.multiple_of(a * H, H)
        acc[m, pl.ds(start, H)] += rb1[m, 0] + rb1[m, 1] + rb1[m, 2]
        sent = []
        for d in range(1, 16):
            piece = pl.ds(pl.multiple_of(start + (by + d) % 16 * 8, 8), 8)
            sent.append(go(acc.at[m, piece], rb2.at[m, d - 1], plane[d - 1]))
        yield
        for copy in sent:
            copy.wait_recv()
        total = acc[m, pl.ds(pl.multiple_of(start + by * 8, 8), 8)] + jnp.sum(rb2[m], axis=0)
        part, base = a // 2, a % 2 * H
        piece = pl.ds(pl.multiple_of(base + by * 8, 8), 8)
        newp[part, m, piece, mine] = probe[part, m, piece, mine] - factor * total
        ref = newp.at[part, m, piece, mine]
        sent = [go(ref, ref, p) for p in plane]
        yield
        for copy in sent:
            copy.wait_recv()
        ref = newp.at[part, m, pl.ds(pl.multiple_of(base, H), H), mine]
        sent = [go(ref, ref, p) for p in line]
        yield
        for copy in sent:
            copy.wait_recv()
        ref = newp.at[:, m, :, mine]
        copy = go(ref, ref, partner)
        yield
        copy.wait_recv()
        yield

    pg[...] = jnp.zeros_like(pg)
    chains = []
    for m in range(MODES):
        for seg in range(2):

            def two(i, carry, m=m, seg=seg):
                s = seg * 4 + i * 2
                inverse(m, [s, s + 1])
                return carry

            lax.fori_loop(0, 2, two, 0)
            for chain in chains:
                next(chain)
        chains.append(probe_sum(m))
        next(chains[-1])

    half_lane = lax.broadcasted_iota(jnp.int32, (8, 8, N), 2)

    def deposit(lo, hi):
        def block(i, carry):
            k, q = i % 2, i // 2
            first, second = 0.0, 0.0
            for s in range(SLOTS):
                at = geo[s * GEO + PLACES + q]
                v = jnp.stack([tall[s, k, at + j] for j in range(8)])
                w = jnp.where(half_lane >= geo[s * GEO + LEFT], v, 0.0)
                first, second = first + w, second + (v - w)
            pad[k, pl.ds(q * 8, 8), :, 0:N] = first
            pad[k, pl.ds(q * 8, 8), :, N : 2 * N] = second
            return carry

        lax.fori_loop(lo // 4, hi // 4, block, 0)

    def turn():
        for chain in chains:
            next(chain, None)

    from_east, from_west = [], []

    def to_cols(lo, hi):
        from_east.append(go(pad.at[:, HT + lo : HT + hi, :, 0:H], from_cols.at[0, :, lo:hi], west))
        from_west.append(go(pad.at[:, HT + lo : HT + hi, :, H + N :], from_cols.at[1, :, lo:hi], east))

    deposit(0, HT)
    deposit(HT + TT, PT)
    from_below = go(pad.at[:, 0:HT], from_rows.at[0], up)
    from_above = go(pad.at[:, HT + TT :], from_rows.at[1], down)
    turn()
    deposit(2 * HT, TT)
    turn()
    to_cols(HT, TT - HT)
    deposit(HT, 2 * HT)
    deposit(TT, TT + HT)
    from_below.wait_recv()
    pad[:, TT : TT + HT] += from_rows[0] * (r < ROWS - 1).astype(F32)
    from_above.wait_recv()
    pad[:, HT : 2 * HT] += from_rows[1] * (r > 0).astype(F32)
    to_cols(0, HT)
    to_cols(TT - HT, TT)
    for _ in range(6):
        turn()
    out[...] -= 0.25 * pad[:, HT : HT + TT, :, H : H + N]
    for copy in from_east:
        copy.wait_recv()
    out[:, :, :, H:N] -= from_cols[0] * ((c < COLS - 1).astype(F32) * 0.25)
    for copy in from_west:
        copy.wait_recv()
    out[:, :, :, 0:H] -= from_cols[1] * ((c > 0).astype(F32) * 0.25)
    for copy in copies_out:
        copy.wait_send()


def on_device(object_field, probe_modes, amplitudes, scan_offsets, slot_counts):
    hbm = pl.BlockSpec(memory_space=pl.ANY)
    sm = pl.BlockSpec(memory_space=pltpu.SMEM)
    vm = pl.BlockSpec(memory_space=pltpu.VMEM)
    new_object, new_probe = pl.pallas_call(
        body,
        out_shape=(
            jax.ShapeDtypeStruct((2, TT, 8, N), F32),
            jax.ShapeDtypeStruct((2, MODES, N, N), F32),
        ),
        in_specs=[sm, sm, hbm, hbm, hbm, hbm, hbm],
        out_specs=(vm, vm),
        scratch_shapes=[
            pltpu.VMEM((2, PT, 8, 2 * N), F32),
            pltpu.VMEM((2, MODES, N, N), F32),
            pltpu.VMEM((SLOTS, N, N), F32),
            pltpu.VMEM((8, N, N), BF16),
            pltpu.VMEM((N, N), BF16),
            pltpu.VMEM((2, N, H), F32),
            pltpu.VMEM((MODES, 2, N, N), F32),
            pltpu.VMEM((SLOTS * MODES * 2, N, N), BF16),
            pltpu.VMEM((SLOTS * MODES * 2, N, N), BF16),
            pltpu.VMEM((SLOTS, 2, N, N), F32),
            pltpu.VMEM((SLOTS, 2, TALL, 8, N), F32),
            pltpu.VMEM((2, 2, HT, 8, 2 * N), F32),
            pltpu.VMEM((2, 2, TT, 8, H), F32),
            pltpu.VMEM((MODES, 2 * N, N), F32),
            pltpu.VMEM((MODES, 2 * N, H), F32),
            pltpu.VMEM((MODES, 2 * N, H), F32),
            pltpu.VMEM((MODES, 3, H, H), F32),
            pltpu.VMEM((MODES, 15, 8, H), F32),
            pltpu.SemaphoreType.DMA((6,)),
            pltpu.SemaphoreType.DMA((2, 12 + 8 + 38 * MODES)),
        ],
        compiler_params=pltpu.CompilerParams(
            collective_id=1, has_side_effects=True, vmem_limit_bytes=58 * 2**20
        ),
        name="step",
    )(
        geometry(scan_offsets),
        slot_counts,
        object_field.reshape(2, TT, 8, N),
        probe_modes,
        amplitudes.reshape(SLOTS, N, N),
        jnp.asarray(tables()),
        jnp.asarray(spread_table()),
    )
    return new_object.reshape(object_field.shape), new_probe


def solution(mesh):
    placed = (
        P(None, "row", "col"),
        P(),
        P("row", "col", None, None, None),
        P("row", "col", None, None),
        P("row", "col"),
    )
    return jax.shard_map(
        on_device,
        mesh=mesh,
        in_specs=placed,
        out_specs=(P(None, "row", "col"), P()),
        check_vma=False,
    )
```

time: 676 us -> 130 us (0.19); the launches traced: 663 us -> 129 us
  matrix products: 234 us -> 0 us
  waiting for transfers between devices: 211 us -> 0 us
  Pallas kernels: 0 us -> 122 us
  local copies, waits for them, and re-layouts: 109 us -> 5.53 us
  other arithmetic: 42.3 us -> 0.88 us
  loops' own time: 31.2 us -> 0 us
  starting transfers between devices: 20.4 us -> 0 us
  between operations: 15.2 us -> 1.32 us
    dot_general x16 -> x0, matrix products: 234 us -> none  [the longest x2 41.9 us: transform(): jnp.einsum('cmkn,nj->cmkj', left_real, sine, precision=highest)]
    pallas_call x0 -> x1, Pallas kernels: none -> 122 us  [on_device(): pl.pallas_call(body, out_shape=(jax.ShapeDtypeStruct((2, TT, 8, N), F32),...]
    psum x1 -> x0, waiting for transfers between devices: 112 us -> none  [on_device(): total = lax.psum(local_probe, ('row', 'col'))]
    ppermute x8 -> x0, waiting for transfers between devices: 99.1 us -> none  [the longest x4 68.1 us: passed_along(): return lax.ppermute(block, axis, route)]
    dynamic_update_slice x8 -> x0, local copies, waits for them, and re-layouts: 52.9 us -> none  [deposit(): return lax.dynamic_update_slice(total, current + patch_grads[slot], start)]
    gather x24 -> x0, local copies, waits for them, and re-layouts: 32.5 us -> none
    another operation x2 -> x0, loops' own time: 31.2 us -> none  [the longest x1 31.1 us: on_device(): gradient = lax.fori_loop(0, capacity, deposit, jnp.zeros_like(padded))]
    ppermute x8 -> x0, starting transfers between devices: 20.3 us -> none  [the longest x2 8.76 us: extended(): before = lax.ppermute(last, axis, up)]
  transfers between devices with their start and end apart: 9 -> 0, of which waited for: 8 -> 0; matrix products, arithmetic and copies ran while one was open for 2% -> 0% of each run, Pallas kernels for 0% -> 0%
where the time goes in v2:
time: 130 us; the launch traced here: 129 us
  Pallas kernels  122 us (94%)
  local copies, waits for them, and re-layouts  5.53 us (4%)
  between operations  1.32 us (1%)
    pallas_call x1, Pallas kernels, on_device(): pl.pallas_call(body, out_shape=(jax.ShapeDtypeStruct((2, TT, 8, N), F32),...  122 us
    unnamed x4, local copies, waits for them, and re-layouts  4.31 us

profile of v2, /device:TPU:1, one launch (start us, length us, event | category | flops | bytes accessed | tf_op | source)
XLA Modules:
  0.0 129.5 jit_solution(7947861323858442469)
XLA Ops:
  1.3 0.8 and_select_fusion
  2.1 0.1 add_clamp_fusion
  2.2 0.1 copy.9
  2.3 0.1 copy.13
  2.3 0.1 copy.11
  2.4 0.1 copy.14
  2.5 0.1 copy.12
  2.6 0.1 copy.10
  2.7 0.1 concatenate.3
  2.8 0.6 reshape.24.geo
  3.4 121.7 %step.1 = (f32[2,128,8,256]{3,2,1,0:T(8,128)}, f32[2,3,256,256]{3,2,1,0:T(8,128)}) custom-call(s32[256]{0:T(256)} %reshape.24.geo, s32[1,1]{1,0:T(1,128)S(6)} %copy.17.cnt, f32[2,128,8,256]{3,2,1,0:T(8,128)} %bitcast.6, f32[2,3,256,256]{3,2,1,0:T(8,128)} %probe_hbm.1, f32[8,256,256]{2,1,0:T(8,128)} %bitcast.7, bf16[8,256,256]{2,1,0:T(8,128)(2,1)} %constant.74.clone.tab_hbm, ...), custom_call_target="tpu_custom_call" | custom-call | tf_op jit(solution)/shard_map/step/pallas_call | solution.py:401
  125.1 0.0 copy-start
  125.2 3.2 %copy.18 = f32[2,1024,256]{2,1,0:T(8,128)} copy(f32[2,1024,256]{2,1,0:T(8,128)} %bitcast.8) | data formatting | bytes 4194304
  128.3 0.0 copy-done
  128.3 1.1 copy.19
  (4 shorter events, 0.0 us)
Async XLA Ops:
  125.1 3.2 %copy-start = (f32[2,3,256,256]{3,2,1,0:T(8,128)S(1)}, f32[2,3,256,256]{3,2,1,0:T(8,128)}, u32[]{:S(2)}) copy-start(f32[2,3,256,256]{3,2,1,0:T(8,128)} %get-tuple-element.19) | copy-start | bytes 4718596

commit v3 on v2

--- a/solution.py
+++ b/solution.py
@@ -86,7 +86,8 @@
 GEO = 32
 FIRST, SHIFT, LEFT, BACK_ROW, BACK_COL, ROW, PLACES = range(7)
 HT, TT, PT = H // 8, T // 8, PAD_R // 8
-TALL = 2 * HT + N // 8 + 1
+EDGE = 8
+TALL = 2 * EDGE + N // 8 + 1
 
 
 def geometry(scan_offsets):
@@ -94,7 +95,7 @@
     top, lft = (off[:, 0] + H) % T, (off[:, 1] + H) % N
     shift = top % 8
     first = top // 8
-    places = jnp.clip(jnp.arange(0, PT, 8)[None] - first[:, None] + HT, 0, TALL - 8)
+    places = jnp.clip(jnp.arange(0, PT, 8)[None] - first[:, None] + EDGE, 0, TALL - 8)
     fixed = jnp.stack([first, shift, lft, (8 - shift) % 8, (N - lft) % N, off[:, 0]], axis=1)
     table = jnp.concatenate([fixed, places], axis=1).astype(jnp.int32)
     return jnp.pad(table, ((0, 0), (0, GEO - table.shape[1]))).reshape(SLOTS * GEO)
@@ -177,8 +178,8 @@
         v = above(*(beside(*(halves[i, pl.ds(o, H, 2), :] for i in range(2))) for o in range(2)))
         vh, vl = split(v)
         amp[s] = jnp.dot(beside(vh, vl), above(spread[...], spread[...]), preferred_element_type=F32)
-        tall[s, :, 0:HT] = jnp.zeros((2, HT, 8, N), F32)
-        tall[s, :, TALL - HT :] = jnp.zeros((2, HT, 8, N), F32)
+        tall[s, :, 0:EDGE] = jnp.zeros((2, EDGE, 8, 2 * N), F32)
+        tall[s, :, TALL - EDGE :] = jnp.zeros((2, EDGE, 8, 2 * N), F32)
         return carry
 
     lax.fori_loop(0, SLOTS, order, 0)
@@ -193,6 +194,7 @@
     lane = lax.broadcasted_iota(jnp.int32, (N, N), 1)
     sub = lax.broadcasted_iota(jnp.int32, (N, N), 0)
     row8 = lax.broadcasted_iota(jnp.int32, (8, N), 0)
+    lane33 = lax.broadcasted_iota(jnp.int32, (N // 8 + 1, 8, N), 2)
     col0 = c * N - H
 
     def forward(s, carry):
@@ -266,14 +268,17 @@
             mode_i = mode_i + (pr * ci - pi * cr)
             grads = (qr * cr + qi * ci, qr * ci - qi * cr)
             for k, g in enumerate(grads):
-                inner = slice(HT, HT + N // 8)
+                inner = slice(EDGE, EDGE + N // 8)
                 if m > 0:
-                    g = g + tall[s, k, inner].reshape(N, N)
+                    g = g + tall[s, k, inner, :, 0:N].reshape(N, N)
                 if m < MODES - 1:
-                    tall[s, k, inner] = g.reshape(N // 8, 8, N)
+                    tall[s, k, inner, :, 0:N] = g.reshape(N // 8, 8, N)
                 else:
-                    g = pltpu.roll(g, geo[s * GEO + LEFT], 1)
-                    tall[s, k, HT : TALL - HT] = rows_down(g, geo[s * GEO + SHIFT], row8)
+                    lft = geo[s * GEO + LEFT]
+                    g = rows_down(pltpu.roll(g, lft, 1), geo[s * GEO + SHIFT], row8)
+                    first = jnp.where(lane33 >= lft, g, 0.0)
+                    tall[s, k, EDGE : TALL - EDGE, :, 0:N] = first
+                    tall[s, k, EDGE : TALL - EDGE, :, N : 2 * N] = g - first
         pg[m, 0:N] += mode_r
         pg[m, N:] += mode_i
 
@@ -338,22 +343,17 @@
         chains.append(probe_sum(m))
         next(chains[-1])
 
-    half_lane = lax.broadcasted_iota(jnp.int32, (8, 8, N), 2)
-
     def deposit(lo, hi):
-        def block(i, carry):
-            k, q = i % 2, i // 2
-            first, second = 0.0, 0.0
-            for s in range(SLOTS):
-                at = geo[s * GEO + PLACES + q]
-                v = jnp.stack([tall[s, k, at + j] for j in range(8)])
-                w = jnp.where(half_lane >= geo[s * GEO + LEFT], v, 0.0)
-                first, second = first + w, second + (v - w)
-            pad[k, pl.ds(q * 8, 8), :, 0:N] = first
-            pad[k, pl.ds(q * 8, 8), :, N : 2 * N] = second
+        def block(q, carry):
+            for k in range(2):
+                total = [0.0] * 8
+                for s in range(SLOTS):
+                    at = geo[s * GEO + PLACES + q]
+                    total = [total[j] + tall[s, k, at + j] for j in range(8)]
+                pad[k, pl.ds(q * 8, 8)] = jnp.stack(total)
             return carry
 
-        lax.fori_loop(lo // 4, hi // 4, block, 0)
+        lax.fori_loop(lo // 8, hi // 8, block, 0)
 
     def turn():
         for chain in chains:
@@ -371,19 +371,22 @@
     from_above = go(pad.at[:, HT + TT :], from_rows.at[1], down)
     turn()
     deposit(2 * HT, TT)
-    turn()
-    to_cols(HT, TT - HT)
+    to_cols(HT, HT + 24)
     deposit(HT, 2 * HT)
     deposit(TT, TT + HT)
+    turn()
+    to_cols(HT + 24, HT + 48)
     from_below.wait_recv()
     pad[:, TT : TT + HT] += from_rows[0] * (r < ROWS - 1).astype(F32)
     from_above.wait_recv()
     pad[:, HT : 2 * HT] += from_rows[1] * (r > 0).astype(F32)
+    turn()
+    to_cols(HT + 48, TT - HT)
     to_cols(0, HT)
     to_cols(TT - HT, TT)
+    out[...] -= 0.25 * pad[:, HT : HT + TT, :, H : H + N]
     for _ in range(6):
         turn()
-    out[...] -= 0.25 * pad[:, HT : HT + TT, :, H : H + N]
     for copy in from_east:
         copy.wait_recv()
     out[:, :, :, H:N] -= from_cols[0] * ((c < COLS - 1).astype(F32) * 0.25)
@@ -417,7 +420,7 @@
             pltpu.VMEM((SLOTS * MODES * 2, N, N), BF16),
             pltpu.VMEM((SLOTS * MODES * 2, N, N), BF16),
             pltpu.VMEM((SLOTS, 2, N, N), F32),
-            pltpu.VMEM((SLOTS, 2, TALL, 8, N), F32),
+            pltpu.VMEM((SLOTS, 2, TALL, 8, 2 * N), F32),
             pltpu.VMEM((2, 2, HT, 8, 2 * N), F32),
             pltpu.VMEM((2, 2, TT, 8, H), F32),
             pltpu.VMEM((MODES, 2 * N, N), F32),
@@ -426,7 +429,7 @@
             pltpu.VMEM((MODES, 3, H, H), F32),
             pltpu.VMEM((MODES, 15, 8, H), F32),
             pltpu.SemaphoreType.DMA((6,)),
-            pltpu.SemaphoreType.DMA((2, 12 + 8 + 38 * MODES)),
+            pltpu.SemaphoreType.DMA((2, 12 + 12 + 38 * MODES)),
         ],
         compiler_params=pltpu.CompilerParams(
             collective_id=1, has_side_effects=True, vmem_limit_bytes=58 * 2**20

time: 130 us -> 130 us (level)
  the two profiles are of different devices: /device:TPU:1 before, /device:TPU:4 now
where the time goes in v3:
time: 130 us
  Pallas kernels  122 us (94%)
  local copies, waits for them, and re-layouts  5.53 us (4%)
  between operations  1.32 us (1%)
    pallas_call x1, Pallas kernels, on_device(): pl.pallas_call(body, out_shape=(jax.ShapeDtypeStruct((2, TT, 8, N), F32),...  122 us
    unnamed x4, local copies, waits for them, and re-layouts  4.31 us

profile of v3, /device:TPU:4, one launch (start us, length us, event | category | flops | bytes accessed | tf_op | source)
XLA Modules:
  0.0 129.6 jit_solution(3706946156896303022)
XLA Ops:
  1.3 0.8 and_select_fusion
  2.1 0.1 add_clamp_fusion
  2.2 0.1 copy.9
  2.3 0.1 copy.13
  2.3 0.1 copy.11
  2.4 0.1 copy.14
  2.5 0.1 copy.12
  2.6 0.1 copy.10
  2.7 0.1 concatenate.3
  2.8 0.6 reshape.24.geo
  3.4 121.9 %step.1 = (f32[2,128,8,256]{3,2,1,0:T(8,128)}, f32[2,3,256,256]{3,2,1,0:T(8,128)}) custom-call(s32[256]{0:T(256)} %reshape.24.geo, s32[1,1]{1,0:T(1,128)S(6)} %copy.17.cnt, f32[2,128,8,256]{3,2,1,0:T(8,128)} %bitcast.6, f32[2,3,256,256]{3,2,1,0:T(8,128)} %probe_hbm.1, f32[8,256,256]{2,1,0:T(8,128)} %bitcast.7, bf16[8,256,256]{2,1,0:T(8,128)(2,1)} %constant.73.clone.tab_hbm, ...), custom_call_target="tpu_custom_call" | custom-call | tf_op jit(solution)/shard_map/step/pallas_call | solution.py:404
  125.3 0.0 copy-start
  125.3 3.2 %copy.18 = f32[2,1024,256]{2,1,0:T(8,128)} copy(f32[2,1024,256]{2,1,0:T(8,128)} %bitcast.8) | data formatting | bytes 4194304
  128.5 0.0 copy-done
  128.5 1.1 copy.19
  (4 shorter events, 0.0 us)
Async XLA Ops:
  125.3 3.2 %copy-start = (f32[2,3,256,256]{3,2,1,0:T(8,128)S(1)}, f32[2,3,256,256]{3,2,1,0:T(8,128)}, u32[]{:S(2)}) copy-start(f32[2,3,256,256]{3,2,1,0:T(8,128)} %get-tuple-element.19) | copy-start | bytes 4718596

commit v4 on v3

v4 whole, which is shorter than its diff:
```python
import math

import jax
import jax.numpy as jnp
import ml_dtypes
import numpy as np
from jax import lax
from jax.experimental import pallas as pl
from jax.experimental.pallas import tpu as pltpu
from jax.sharding import PartitionSpec as P

N = 256
H = 128
MODES = 3
PAD_R = 1280
T = 1024
SLOTS = 8
ROWS, COLS = 8, 16
MESH = pl.DeviceIdType.MESH
F32 = jnp.float32
BF16 = jnp.bfloat16
OBJ_R = 8192
OBJ_C = 4096


def tables():
    n = np.arange(H)[:, None]
    k = np.arange(H)[None, :]
    out = []
    for odd in (0, 1):
        angle = 2.0 * np.pi * ((n * (2 * k + odd)) % N) / N
        c, s = np.cos(angle) / 16.0, np.sin(angle) / 16.0
        full = np.block([[c, -s], [s, c]])
        for matrix in (full, full.T):
            high = matrix.astype(ml_dtypes.bfloat16)
            low = (matrix - high.astype(np.float64)).astype(ml_dtypes.bfloat16)
            out += [high, low]
    return np.stack(out)


def spread_table():
    matrix = np.zeros((N, N), np.float32)
    matrix[np.arange(0, N, 2), np.arange(H)] = 1.0
    matrix[np.arange(1, N, 2), np.arange(H) + H] = 1.0
    return matrix.astype(ml_dtypes.bfloat16)


def split(x):
    high = x.astype(BF16)
    return high, (x - high.astype(F32)).astype(BF16)


def right(pair, high, low):
    xh, xl = pair
    return jnp.dot(
        jnp.concatenate([xh, xl, xh], axis=1), jnp.concatenate([high, high, low], axis=0), preferred_element_type=F32
    )


def left(high, low, pair):
    xh, xl = pair
    return jnp.dot(
        jnp.concatenate([high, low, high], axis=1), jnp.concatenate([xh, xh, xl], axis=0), preferred_element_type=F32
    )


def beside(a, b):
    return jnp.concatenate([a, b], axis=1)


def above(a, b):
    return jnp.concatenate([a, b], axis=0)


def rows_up(tiles, shift, back, row8):
    t = [pltpu.roll(v, back, 0) for v in tiles]
    return jnp.concatenate([jnp.where(row8 < 8 - shift, p, q) for p, q in zip(t[:-1], t[1:])], axis=0)


def rows_down(v, shift, row8):
    t = pltpu.roll(v.reshape(N // 8, 8, N), shift, 1)
    none = jnp.zeros((1, 8, N), F32)
    return jnp.where(row8[None] >= shift, jnp.concatenate([t, none], axis=0), jnp.concatenate([none, t], axis=0))


GEO = 32
FIRST, SHIFT, LEFT, BACK_ROW, BACK_COL, ROW, PLACES = range(7)
HT, TT, PT = H // 8, T // 8, PAD_R // 8
EDGE = 8
TALL = 2 * EDGE + N // 8 + 1


def geometry(scan_offsets):
    off = scan_offsets.reshape(SLOTS, 2)
    top, lft = (off[:, 0] + H) % T, (off[:, 1] + H) % N
    shift = top % 8
    first = top // 8
    places = jnp.clip(jnp.arange(0, PT, 8)[None] - first[:, None] + EDGE, 0, TALL - 8)
    fixed = jnp.stack([first, shift, lft, (8 - shift) % 8, (N - lft) % N, off[:, 0]], axis=1)
    table = jnp.concatenate([fixed, places], axis=1).astype(jnp.int32)
    return jnp.pad(table, ((0, 0), (0, GEO - table.shape[1]))).reshape(SLOTS * GEO)


def body(
    geo, cnt, obj, obj_flat, probe_hbm, amp_hbm, tab_hbm, spread_hbm,
    out, newp,
    pad, probe, tab, spread, halves, spec_a, spec_b, wave_a, wave_b, sh, sl, patch, tall, from_rows, from_cols,
    pg, half, rb1, rb2, rb3, local, sems,
):
    r, c = lax.axis_index("row"), lax.axis_index("col")
    up, down = ((r + ROWS - 1) % ROWS, c), ((r + 1) % ROWS, c)
    west, east = (r, (c + COLS - 1) % COLS), (r, (c + 1) % COLS)
    x, core, z, y = r // 2, r % 2, c // 4, c % 4
    partner = (x * 2 + 1 - core, c)
    a, b = x, z

    def dev(a_, b_, y_):
        return (a_ * 2 + core, b_ * 4 + y_)

    line_a = [dev((a + d) % 4, b, y) for d in range(1, 4)]
    line_b = [dev(a, (b + d) % 4, y) for d in range(1, 4)]
    line_y = [dev(a, b, (y + d) % 4) for d in range(1, 4)]

    fetch = [
        pltpu.make_async_copy(src, dst, local.at[i])
        for i, (src, dst) in enumerate(
            (
                (obj, pad.at[:, HT : HT + TT, :, H : H + N]),
                (amp_hbm, out),
                (spread_hbm, spread),
                (probe_hbm, probe),
                (tab_hbm, tab),
            )
        )
    ]
    for f in fetch:
        f.start()

    peers = line_a + line_b + line_y + [up, down, west, east]
    barrier = pltpu.get_barrier_semaphore()
    for p in peers:
        pl.semaphore_signal(barrier, inc=1, device_id=p, device_id_type=MESH)
    pl.semaphore_wait(barrier, len(peers))

    count, copies_out = [0], []

    def go(src, dst, where):
        i = count[0]
        count[0] += 1
        copy = pltpu.make_async_remote_copy(
            src_ref=src, dst_ref=dst, send_sem=sems.at[0, i], recv_sem=sems.at[1, i], device_id=where, device_id_type=MESH
        )
        copy.start()
        copies_out.append(copy)
        return copy

    cols = []
    for lo, hi in ((0, HT), (TT - HT, TT), (HT, TT - HT)):
        cols.append(go(obj.at[:, lo:hi, :, H:N], pad.at[:, HT + lo : HT + hi, :, 0:H], east))
        cols.append(go(obj.at[:, lo:hi, :, 0:H], pad.at[:, HT + lo : HT + hi, :, H + N :], west))
    rows = [
        go(obj.at[:, TT - HT : TT], pad.at[:, 0:HT, :, H : H + N], down),
        go(obj.at[:, 0:HT], pad.at[:, HT + TT :, :, H : H + N], up),
    ]
    for k, lanes in ((0, slice(0, H)), (1, slice(H + N, 2 * N))):
        cols[k].wait_recv()
        rows.append(go(pad.at[:, HT : 2 * HT, :, lanes], pad.at[:, HT + TT :, :, lanes], up))
        cols[2 + k].wait_recv()
        rows.append(go(pad.at[:, TT : TT + HT, :, lanes], pad.at[:, 0:HT, :, lanes], down))

    fetch[1].wait()
    fetch[2].wait()

    def order(s, carry):
        halves[0] = out[s, :, 0:H]
        halves[1] = out[s, :, H:N]
        v = above(*(beside(*(halves[i, pl.ds(o, H, 2), :] for i in range(2))) for o in range(2)))
        vh, vl = split(v)
        out[s] = jnp.dot(beside(vh, vl), above(spread[...], spread[...]), preferred_element_type=F32)
        tall[s] = jnp.zeros((2, TALL, 8, 2 * N), F32)
        return carry

    lax.fori_loop(0, SLOTS, order, 0)
    for f in (fetch[0], fetch[3], fetch[4]):
        f.wait()
    for copy in rows + cols[4:]:
        copy.wait_recv()
    for copy in rows + cols:
        copy.wait_send()
    del copies_out[:]

    lane = lax.broadcasted_iota(jnp.int32, (N, N), 1)
    sub = lax.broadcasted_iota(jnp.int32, (N, N), 0)
    row8 = lax.broadcasted_iota(jnp.int32, (8, N), 0)
    lane33 = lax.broadcasted_iota(jnp.int32, (N // 8 + 1, 8, N), 2)
    col0 = c * N - H

    def window(s, wave):
        g = s * GEO
        first, shift, lft = geo[g + FIRST], geo[g + SHIFT], geo[g + LEFT]
        row = sub + geo[g + ROW]
        row_ok = (row >= 0) & (row < OBJ_R)
        ok_first = row_ok & (lane >= lft) & (lane + col0 >= 0)
        ok_second = row_ok & (lane < lft) & (lane + (col0 + N) < OBJ_C)
        parts = []
        for i in range(2):
            sides = []
            for lanes in (slice(0, N), slice(N, 2 * N)):
                tiles = [pad[i, first + k, :, lanes] for k in range(N // 8 + 1)]
                sides.append(rows_up(tiles, shift, geo[g + BACK_ROW], row8))
            v = jnp.where(ok_first, sides[0], jnp.where(ok_second, sides[1], 0.0))
            parts.append(pltpu.roll(v, geo[g + BACK_COL], 1))
        pr, pi = parts
        patch[s, 0] = pr
        patch[s, 1] = pi
        for m in range(MODES):
            qr, qi = probe[0, m], probe[1, m]
            wr = qr * pr - qi * pi
            wi = qr * pi + qi * pr
            rows = slice(m * N, (m + 1) * N)
            plus = beside(wr[:, :H] + wr[:, H:], wi[:, :H] + wi[:, H:])
            wave[0, 0, rows], wave[0, 1, rows] = split(plus)
            minus = beside(wr[:, :H] - wr[:, H:], wi[:, :H] - wi[:, H:])
            wave[1, 0, rows], wave[1, 1, rows] = split(minus)

    def transform(wave, spec):
        ye = right((wave[0, 0], wave[0, 1]), tab[0], tab[1])
        yo = right((wave[1, 0], wave[1, 1]), tab[4], tab[5])
        for m in range(MODES):
            k = m * N
            for i, sign in enumerate((1.0, -1.0)):
                e = ye[k : k + H] + sign * ye[k + H : k + N]
                o = yo[k : k + H] + sign * yo[k + H : k + N]
                part = above(beside(e[:, :H], o[:, :H]), beside(e[:, H:], o[:, H:]))
                spec[m, i] = left(tab[2 + 4 * i], tab[3 + 4 * i], split(part))

    def scale(s, spec):
        live = jnp.where(s < cnt[0, 0], 1.0, 0.0)
        for i in range(2):
            power = 0.0
            for m in range(MODES):
                v = spec[m, i]
                power = power + (v[:H] * v[:H] + v[H:] * v[H:])
            ratio = live * (1.0 - out[s, i * H : (i + 1) * H] * lax.rsqrt(jnp.maximum(power, 1.0)))
            ratio = above(ratio, ratio)
            for m in range(MODES):
                k = (s * MODES + m) * 2 + i
                sh[k], sl[k] = split(spec[m, i] * ratio)

    def two_slots(q, carry):
        s = 2 * q
        transform(wave_a, spec_a)
        window(s + 1, wave_b)
        scale((s + SLOTS - 1) % SLOTS, spec_b)
        transform(wave_b, spec_b)
        window((s + 2) % SLOTS, wave_a)
        scale(s, spec_a)
        return carry

    spec_b[...] = jnp.zeros_like(spec_b)
    window(0, wave_a)
    lax.fori_loop(0, SLOTS // 2, two_slots, 0)
    scale(SLOTS - 1, spec_b)
    again = pltpu.make_async_copy(obj_flat, out, local.at[5])
    again.start()

    PAIRS = SLOTS // 2

    def back(p, spec):
        m, j = p // PAIRS, p % PAIRS
        even, odd = [], []
        for t in range(2):
            k = ((2 * j + t) * MODES + m) * 2
            e = left(tab[0], tab[1], (sh[k], sl[k]))
            o = left(tab[4], tab[5], (sh[k + 1], sl[k + 1]))
            lo, hi = e + o, e - o
            even += [beside(lo[:H, :H], lo[H:, :H]), beside(hi[:H, :H], hi[H:, :H])]
            odd += [beside(lo[:H, H:], lo[H:, H:]), beside(hi[:H, H:], hi[H:, H:])]
        e = right(split(jnp.concatenate(even, axis=0)), tab[2], tab[3])
        o = right(split(jnp.concatenate(odd, axis=0)), tab[6], tab[7])
        for t in range(2):
            spec[t, 0] = e[t * N : (t + 1) * N]
            spec[t, 1] = o[t * N : (t + 1) * N]

    inner = slice(EDGE, EDGE + N // 8)

    def collect(p, spec):
        m, j = p // PAIRS, p % PAIRS
        mode_r, mode_i = 0.0, 0.0
        qr, qi = probe[0, m], probe[1, m]
        for t in range(2):
            s = 2 * j + t
            ee, oo = spec[t, 0], spec[t, 1]
            lo, hi = ee + oo, ee - oo
            cr = beside(lo[:, :H], hi[:, :H])
            ci = beside(lo[:, H:], hi[:, H:])
            pr, pi = patch[s, 0], patch[s, 1]
            mode_r = mode_r + (pr * cr + pi * ci)
            mode_i = mode_i + (pr * ci - pi * cr)
            for k, g in enumerate((qr * cr + qi * ci, qr * ci - qi * cr)):
                tall[s, k, inner, :, 0:N] += g.reshape(N // 8, 8, N)
        pg[m, 0:N] += mode_r
        pg[m, N:] += mode_i

    def settle(s, carry):
        lft = geo[s * GEO + LEFT]
        for k in range(2):
            g = pltpu.roll(tall[s, k, inner, :, 0:N].reshape(N, N), lft, 1)
            g = rows_down(g, geo[s * GEO + SHIFT], row8)
            first = jnp.where(lane33 >= lft, g, 0.0)
            tall[s, k, EDGE : TALL - EDGE, :, 0:N] = first
            tall[s, k, EDGE : TALL - EDGE, :, N : 2 * N] = g - first
        return carry

    mine = pl.ds(pl.multiple_of(core * H, H), H)
    other = pl.ds(pl.multiple_of((1 - core) * H, H), H)
    factor = 0.5 / math.sqrt(ROWS * COLS * SLOTS)

    def probe_sum(ms):
        copy = go(pg.at[ms, :, other], half.at[ms], partner)
        yield
        copy.wait_recv()
        half[ms] += pg[ms, :, mine]
        start = 0
        for peers, at, buf, size in ((line_a, a, rb1, H), (line_b, b, rb2, H // 4), (line_y, y, rb3, 8)):
            sent = []
            for d in range(1, 4):
                piece = pl.ds(pl.multiple_of(start + (at + d) % 4 * size, 8), size)
                sent.append(go(half.at[ms, piece], buf.at[d - 1, ms], peers[d - 1]))
            yield
            start = start + at * size
            for copy in sent:
                copy.wait_recv()
            half[ms, pl.ds(pl.multiple_of(start, 8), size)] += buf[0, ms] + buf[1, ms] + buf[2, ms]
        part, base = a // 2, a % 2 * H
        base = base + b * (H // 4)
        piece = pl.ds(pl.multiple_of(base + y * 8, 8), 8)
        newp[part, ms, piece, mine] = probe[part, ms, piece, mine] - factor * half[ms, pl.ds(pl.multiple_of(start, 8), 8)]
        for peers, at, size in ((line_y, base + y * 8, 8), (line_b, base, H // 4), (line_a, a % 2 * H, H)):
            ref = newp.at[part, ms, pl.ds(pl.multiple_of(at, 8), size), mine]
            sent = [go(ref, ref, p) for p in peers]
            yield
            for copy in sent:
                copy.wait_recv()
        ref = newp.at[:, ms, :, mine]
        copy = go(ref, ref, partner)
        yield
        copy.wait_recv()

    pg[...] = jnp.zeros_like(pg)
    chains = []

    def begin(ms):
        chains.append(probe_sum(ms))
        next(chains[-1])

    def turn():
        for chain in chains:
            next(chain, None)

    def two_pairs(q, carry):
        p = 2 * q
        back(p + 1, spec_b)
        collect(p, spec_a)
        back(p + 2, spec_a)
        collect(p + 1, spec_b)
        return carry

    back(0, spec_a)
    lax.fori_loop(0, PAIRS, two_pairs, 0)
    begin(slice(0, 2))
    lax.fori_loop(PAIRS, PAIRS + 1, two_pairs, 0)
    turn()
    back(3 * PAIRS - 1, spec_b)
    collect(3 * PAIRS - 2, spec_a)
    collect(3 * PAIRS - 1, spec_b)
    begin(slice(2, 3))
    turn()
    lax.fori_loop(0, SLOTS, settle, 0)

    def deposit(lo, hi):
        def block(q, carry):
            for k in range(2):
                total = [0.0] * 8
                for s in range(SLOTS):
                    at = geo[s * GEO + PLACES + q]
                    total = [total[j] + tall[s, k, at + j] for j in range(8)]
                pad[k, pl.ds(q * 8, 8)] = jnp.stack(total)
            return carry

        lax.fori_loop(lo // 8, hi // 8, block, 0)

    from_east, from_west = [], []

    def to_cols(lo, hi):
        from_east.append(go(pad.at[:, HT + lo : HT + hi, :, 0:H], from_cols.at[0, :, lo:hi], west))
        from_west.append(go(pad.at[:, HT + lo : HT + hi, :, H + N :], from_cols.at[1, :, lo:hi], east))

    deposit(0, HT)
    deposit(HT + TT, PT)
    from_below = go(pad.at[:, 0:HT], from_rows.at[0], up)
    from_above = go(pad.at[:, HT + TT :], from_rows.at[1], down)
    turn()
    deposit(2 * HT, TT)
    to_cols(HT, HT + 24)
    deposit(HT, 2 * HT)
    deposit(TT, TT + HT)
    turn()
    to_cols(HT + 24, HT + 48)
    from_below.wait_recv()
    pad[:, TT : TT + HT] += from_rows[0] * (r < ROWS - 1).astype(F32)
    from_above.wait_recv()
    pad[:, HT : 2 * HT] += from_rows[1] * (r > 0).astype(F32)
    turn()
    to_cols(HT + 48, HT + 72)
    turn()
    to_cols(HT + 72, TT - HT)
    to_cols(0, HT)
    to_cols(TT - HT, TT)
    again.wait()
    out[...] -= 0.25 * pad[:, HT : HT + TT, :, H : H + N].reshape(SLOTS, N, N)
    for _ in range(8):
        turn()
    for copy in from_east:
        copy.wait_recv()
    out[:, :, H:N] -= (from_cols[0] * ((c < COLS - 1).astype(F32) * 0.25)).reshape(SLOTS, N, H)
    for copy in from_west:
        copy.wait_recv()
    out[:, :, 0:H] -= (from_cols[1] * ((c > 0).astype(F32) * 0.25)).reshape(SLOTS, N, H)
    for copy in copies_out:
        copy.wait_send()


def on_device(object_field, probe_modes, amplitudes, scan_offsets, slot_counts):
    hbm = pl.BlockSpec(memory_space=pl.ANY)
    sm = pl.BlockSpec(memory_space=pltpu.SMEM)
    vm = pl.BlockSpec(memory_space=pltpu.VMEM)
    new_object, new_probe = pl.pallas_call(
        body,
        out_shape=(
            jax.ShapeDtypeStruct((SLOTS, N, N), F32),
            jax.ShapeDtypeStruct((2, MODES, N, N), F32),
        ),
        in_specs=[sm, sm, hbm, hbm, hbm, hbm, hbm, hbm],
        out_specs=(vm, vm),
        scratch_shapes=[
            pltpu.VMEM((2, PT, 8, 2 * N), F32),
            pltpu.VMEM((2, MODES, N, N), F32),
            pltpu.VMEM((8, N, N), BF16),
            pltpu.VMEM((N, N), BF16),
            pltpu.VMEM((2, N, H), F32),
            pltpu.VMEM((MODES, 2, N, N), F32),
            pltpu.VMEM((MODES, 2, N, N), F32),
            pltpu.VMEM((2, 2, MODES * N, N), BF16),
            pltpu.VMEM((2, 2, MODES * N, N), BF16),
            pltpu.VMEM((SLOTS * MODES * 2, N, N), BF16),
            pltpu.VMEM((SLOTS * MODES * 2, N, N), BF16),
            pltpu.VMEM((SLOTS, 2, N, N), F32),
            pltpu.VMEM((SLOTS, 2, TALL, 8, 2 * N), F32),
            pltpu.VMEM((2, 2, HT, 8, 2 * N), F32),
            pltpu.VMEM((2, 2, TT, 8, H), F32),
            pltpu.VMEM((MODES, 2 * N, N), F32),
            pltpu.VMEM((MODES, 2 * N, H), F32),
            pltpu.VMEM((3, MODES, H, H), F32),
            pltpu.VMEM((3, MODES, H // 4, H), F32),
            pltpu.VMEM((3, MODES, 8, H), F32),
            pltpu.SemaphoreType.DMA((6,)),
            pltpu.SemaphoreType.DMA((2, 12 + 14 + 20 * 2)),
        ],
        compiler_params=pltpu.CompilerParams(
            collective_id=1, has_side_effects=True, vmem_limit_bytes=60 * 2**20
        ),
        name="step",
    )(
        geometry(scan_offsets),
        slot_counts,
        object_field.reshape(2, TT, 8, N),
        object_field.reshape(SLOTS, N, N),
        probe_modes,
        amplitudes.reshape(SLOTS, N, N),
        jnp.asarray(tables()),
        jnp.asarray(spread_table()),
    )
    return new_object.reshape(object_field.shape), new_probe


def solution(mesh):
    placed = (
        P(None, "row", "col"),
        P(),
        P("row", "col", None, None, None),
        P("row", "col", None, None),
        P("row", "col"),
    )
    return jax.shard_map(
        on_device,
        mesh=mesh,
        in_specs=placed,
        out_specs=(P(None, "row", "col"), P()),
        check_vma=False,
    )
```

time: 130 us -> 129 us (level)
  the two profiles are of different devices: /device:TPU:4 before, /device:TPU:1 now
where the time goes in v4:
time: 129 us
  Pallas kernels  121 us (94%)
  local copies, waits for them, and re-layouts  5.53 us (4%)
  between operations  1.32 us (1%)
    pallas_call x1, Pallas kernels, on_device(): pl.pallas_call(body, out_shape=(jax.ShapeDtypeStruct((SLOTS, N, N), F32),...  121 us
    unnamed x4, local copies, waits for them, and re-layouts  4.31 us

profile of v4, /device:TPU:1, one launch (start us, length us, event | category | flops | bytes accessed | tf_op | source)
XLA Modules:
  0.0 128.7 jit_solution(2991420431081594447)
XLA Ops:
  1.3 0.8 and_select_fusion
  2.1 0.1 add_clamp_fusion
  2.2 0.1 copy.9
  2.3 0.1 copy.13
  2.3 0.1 copy.11
  2.4 0.1 copy.14
  2.5 0.1 copy.12
  2.6 0.1 copy.10
  2.7 0.1 concatenate.3
  2.8 0.6 reshape.27.geo
  3.4 121.0 %step.1 = (f32[8,256,256]{2,1,0:T(8,128)}, f32[2,3,256,256]{3,2,1,0:T(8,128)}) custom-call(s32[256]{0:T(256)} %reshape.27.geo, s32[1,1]{1,0:T(1,128)S(6)} %copy.17.cnt, f32[2,128,8,256]{3,2,1,0:T(8,128)} %bitcast.7, f32[8,256,256]{2,1,0:T(8,128)} %bitcast.8, f32[2,3,256,256]{3,2,1,0:T(8,128)} %probe_hbm.1, f32[8,256,256]{2,1,0:T(8,128)} %bitcast.9, ...), custom_call_target="tpu_custom_call" | custom-call | tf_op jit(solution)/shard_map/step/pallas_call | solution.py:438
  124.4 0.0 copy-start
  124.4 3.2 %copy.18 = f32[2,1024,256]{2,1,0:T(8,128)} copy(f32[2,1024,256]{2,1,0:T(8,128)} %bitcast.10) | data formatting | bytes 4194304
  127.5 0.0 copy-done
  127.5 1.1 copy.19
  (4 shorter events, 0.0 us)
Async XLA Ops:
  124.4 3.2 %copy-start = (f32[2,3,256,256]{3,2,1,0:T(8,128)S(1)}, f32[2,3,256,256]{3,2,1,0:T(8,128)}, u32[]{:S(2)}) copy-start(f32[2,3,256,256]{3,2,1,0:T(8,128)} %get-tuple-element.19) | copy-start | bytes 4718596

commit v5 on v4

--- a/solution.py
+++ b/solution.py
@@ -322,7 +322,7 @@
         copy.wait_recv()
         half[ms] += pg[ms, :, mine]
         start = 0
-        for peers, at, buf, size in ((line_a, a, rb1, H), (line_b, b, rb2, H // 4), (line_y, y, rb3, 8)):
+        for peers, at, buf, size in ((line_b, b, rb1, H), (line_a, a, rb2, H // 4), (line_y, y, rb3, 8)):
             sent = []
             for d in range(1, 4):
                 piece = pl.ds(pl.multiple_of(start + (at + d) % 4 * size, 8), size)
@@ -332,16 +332,22 @@
             for copy in sent:
                 copy.wait_recv()
             half[ms, pl.ds(pl.multiple_of(start, 8), size)] += buf[0, ms] + buf[1, ms] + buf[2, ms]
-        part, base = a // 2, a % 2 * H
-        base = base + b * (H // 4)
+        part, base = b // 2, b % 2 * H + a * (H // 4)
         piece = pl.ds(pl.multiple_of(base + y * 8, 8), 8)
         newp[part, ms, piece, mine] = probe[part, ms, piece, mine] - factor * half[ms, pl.ds(pl.multiple_of(start, 8), 8)]
-        for peers, at, size in ((line_y, base + y * 8, 8), (line_b, base, H // 4), (line_a, a % 2 * H, H)):
+        for peers, at, size in ((line_y, base + y * 8, 8), (line_b, base, H // 4)):
             ref = newp.at[part, ms, pl.ds(pl.multiple_of(at, 8), size), mine]
             sent = [go(ref, ref, p) for p in peers]
             yield
             for copy in sent:
                 copy.wait_recv()
+        sent = []
+        for low in range(0, N, H):
+            ref = newp.at[:, ms, pl.ds(pl.multiple_of(low + a * (H // 4), 8), H // 4), mine]
+            sent += [go(ref, ref, p) for p in line_a]
+        yield
+        for copy in sent:
+            copy.wait_recv()
         ref = newp.at[:, ms, :, mine]
         copy = go(ref, ref, partner)
         yield
@@ -465,7 +471,7 @@
             pltpu.VMEM((3, MODES, H // 4, H), F32),
             pltpu.VMEM((3, MODES, 8, H), F32),
             pltpu.SemaphoreType.DMA((6,)),
-            pltpu.SemaphoreType.DMA((2, 12 + 14 + 20 * 2)),
+            pltpu.SemaphoreType.DMA((2, 12 + 14 + 23 * 2)),
         ],
         compiler_params=pltpu.CompilerParams(
             collective_id=1, has_side_effects=True, vmem_limit_bytes=60 * 2**20

time: 129 us -> 130 us (level)
  no operation moved by 1% of the time
where the time goes in v5:
time: 130 us
  Pallas kernels  122 us (94%)
  local copies, waits for them, and re-layouts  5.53 us (4%)
  between operations  1.32 us (1%)
    pallas_call x1, Pallas kernels, on_device(): pl.pallas_call(body, out_shape=(jax.ShapeDtypeStruct((SLOTS, N, N), F32),...  122 us
    unnamed x4, local copies, waits for them, and re-layouts  4.31 us

profile of v5, /device:TPU:1, one launch (start us, length us, event | category | flops | bytes accessed | tf_op | source)
XLA Modules:
  0.0 129.8 jit_solution(16207659049863718014)
XLA Ops:
  1.3 0.8 and_select_fusion
  2.1 0.1 add_clamp_fusion
  2.2 0.1 copy.9
  2.3 0.1 copy.13
  2.3 0.1 copy.11
  2.4 0.1 copy.14
  2.5 0.1 copy.12
  2.6 0.1 copy.10
  2.7 0.1 concatenate.3
  2.8 0.6 reshape.27.geo
  3.4 122.1 %step.1 = (f32[8,256,256]{2,1,0:T(8,128)}, f32[2,3,256,256]{3,2,1,0:T(8,128)}) custom-call(s32[256]{0:T(256)} %reshape.27.geo, s32[1,1]{1,0:T(1,128)S(6)} %copy.17.cnt, f32[2,128,8,256]{3,2,1,0:T(8,128)} %bitcast.7, f32[8,256,256]{2,1,0:T(8,128)} %bitcast.8, f32[2,3,256,256]{3,2,1,0:T(8,128)} %probe_hbm.1, f32[8,256,256]{2,1,0:T(8,128)} %bitcast.9, ...), custom_call_target="tpu_custom_call" | custom-call | tf_op jit(solution)/shard_map/step/pallas_call | solution.py:444
  125.5 0.0 copy-start
  125.5 3.2 %copy.18 = f32[2,1024,256]{2,1,0:T(8,128)} copy(f32[2,1024,256]{2,1,0:T(8,128)} %bitcast.10) | data formatting | bytes 4194304
  128.7 0.0 copy-done
  128.7 1.1 copy.19
  (4 shorter events, 0.0 us)
Async XLA Ops:
  125.5 3.2 %copy-start = (f32[2,3,256,256]{3,2,1,0:T(8,128)S(1)}, f32[2,3,256,256]{3,2,1,0:T(8,128)}, u32[]{:S(2)}) copy-start(f32[2,3,256,256]{3,2,1,0:T(8,128)} %get-tuple-element.19) | copy-start | bytes 4718596

commit v6 on v4

--- a/solution.py
+++ b/solution.py
@@ -112,10 +112,10 @@
     west, east = (r, (c + COLS - 1) % COLS), (r, (c + 1) % COLS)
     x, core, z, y = r // 2, r % 2, c // 4, c % 4
     partner = (x * 2 + 1 - core, c)
-    a, b = x, z
+    a, b = x + core * (z - x), z + core * (x - z)
 
     def dev(a_, b_, y_):
-        return (a_ * 2 + core, b_ * 4 + y_)
+        return ((a_ + core * (b_ - a_)) * 2 + core, (b_ + core * (a_ - b_)) * 4 + y_)
 
     line_a = [dev((a + d) % 4, b, y) for d in range(1, 4)]
     line_b = [dev(a, (b + d) % 4, y) for d in range(1, 4)]
@@ -406,13 +406,11 @@
     deposit(HT, 2 * HT)
     deposit(TT, TT + HT)
     turn()
-    to_cols(HT + 24, HT + 48)
+    to_cols(HT + 24, HT + 72)
     from_below.wait_recv()
     pad[:, TT : TT + HT] += from_rows[0] * (r < ROWS - 1).astype(F32)
     from_above.wait_recv()
     pad[:, HT : 2 * HT] += from_rows[1] * (r > 0).astype(F32)
-    turn()
-    to_cols(HT + 48, HT + 72)
     turn()
     to_cols(HT + 72, TT - HT)
     to_cols(0, HT)
@@ -465,7 +463,7 @@
             pltpu.VMEM((3, MODES, H // 4, H), F32),
             pltpu.VMEM((3, MODES, 8, H), F32),
             pltpu.SemaphoreType.DMA((6,)),
-            pltpu.SemaphoreType.DMA((2, 12 + 14 + 20 * 2)),
+            pltpu.SemaphoreType.DMA((2, 12 + 12 + 20 * 2)),
         ],
         compiler_params=pltpu.CompilerParams(
             collective_id=1, has_side_effects=True, vmem_limit_bytes=60 * 2**20

time: 129 us -> 128 us (level)
  no operation moved by 1% of the time
where the time goes in v6:
time: 128 us
  Pallas kernels  120 us (94%)
  local copies, waits for them, and re-layouts  5.53 us (4%)
  between operations  1.32 us (1%)
    pallas_call x1, Pallas kernels, on_device(): pl.pallas_call(body, out_shape=(jax.ShapeDtypeStruct((SLOTS, N, N), F32),...  120 us
    unnamed x4, local copies, waits for them, and re-layouts  4.31 us

profile of v6, /device:TPU:1, one launch (start us, length us, event | category | flops | bytes accessed | tf_op | source)
XLA Modules:
  0.0 127.9 jit_solution(4810042548982302859)
XLA Ops:
  1.3 0.8 and_select_fusion
  2.1 0.1 add_clamp_fusion
  2.2 0.1 copy.9
  2.3 0.1 copy.13
  2.3 0.1 copy.11
  2.4 0.1 copy.14
  2.5 0.1 copy.12
  2.6 0.1 copy.10
  2.7 0.1 concatenate.3
  2.8 0.6 reshape.27.geo
  3.4 120.1 %step.1 = (f32[8,256,256]{2,1,0:T(8,128)}, f32[2,3,256,256]{3,2,1,0:T(8,128)}) custom-call(s32[256]{0:T(256)} %reshape.27.geo, s32[1,1]{1,0:T(1,128)S(6)} %copy.17.cnt, f32[2,128,8,256]{3,2,1,0:T(8,128)} %bitcast.7, f32[8,256,256]{2,1,0:T(8,128)} %bitcast.8, f32[2,3,256,256]{3,2,1,0:T(8,128)} %probe_hbm.1, f32[8,256,256]{2,1,0:T(8,128)} %bitcast.9, ...), custom_call_target="tpu_custom_call" | custom-call | tf_op jit(solution)/shard_map/step/pallas_call | solution.py:436
  123.5 0.0 copy-start
  123.6 3.2 %copy.18 = f32[2,1024,256]{2,1,0:T(8,128)} copy(f32[2,1024,256]{2,1,0:T(8,128)} %bitcast.10) | data formatting | bytes 4194304
  126.7 0.0 copy-done
  126.7 1.1 copy.19
  (4 shorter events, 0.0 us)
Async XLA Ops:
  123.5 3.2 %copy-start = (f32[2,3,256,256]{3,2,1,0:T(8,128)S(1)}, f32[2,3,256,256]{3,2,1,0:T(8,128)}, u32[]{:S(2)}) copy-start(f32[2,3,256,256]{3,2,1,0:T(8,128)} %get-tuple-element.19) | copy-start | bytes 4718596
